TPU v7x, 128 devices: a whole 4x4x4 slice. The times are simulated.
128 devices in a mesh: slot: 4 (over x_hi, core), ctx: 32 (over z, x_lo, y).
Axes of the slice: x: 4 (x_hi: 2, x_lo: 2; x = x_hi * 2 + x_lo), y: 4, z: 4, core: 2. Of those that a mesh axis runs over, the one named last changes fastest.
Arguments:
- latents: bfloat16 [4, 2048, 3072], P('slot', 'ctx'), may hold values from -6 to 6
- fresh: bfloat16 [2048, 3072], P('ctx'), may hold values from -6 to 6
- span_ids: int32 [4], replicated, may hold values from 0 to 3, each once
- noise_step: int32 [4], replicated, may hold values from 0 to 1
- ada_table: float32 [9, 3, 3072], replicated, may hold values from -3 to 3
- w_qkv: bfloat16 [3072, 5120], P(None, 'slot'), may hold values from -1 to 1
- w_out: bfloat16 [3072, 3072], P(None, 'slot'), may hold values from -0.109375 to 0.109375
Outputs:
- velocity: bfloat16 [2, 4, 2048, 3072], P(None, 'slot', 'ctx')
- finished: bfloat16 [2048, 3072], P('ctx', 'slot')
Inputs may be any that keep to these rules, and one draw needn't show every extreme that they name: `span_ids`: each slot holds another span number.
All inputs are finite; a program needn't handle non-finite values.
Results may differ from a plain program's by a relative error of at most 0.02.
Values may be sent and summed in bfloat16 or wider, within the bound.
No kernel may reach another device: no remote copies, remote signals or barrier semaphores. Data moves between devices by JAX's collectives and lax.ppermute only.
A program may use at most 128 MiB of HBM per device.

v0:
```python
import math

import jax
import jax.numpy as jnp
from jax import lax
from jax.sharding import PartitionSpec as P

HEADS = 24
KV_GROUPS = 8
HD = 128
PER = 2


EPS = 1e-06
NEG = -1e30


def from_root(block, axis, holder):
    block = jnp.where(lax.axis_index(axis) == holder, block, jnp.zeros_like(block))
    return lax.psum(block, axis)


def shards(latents, fresh, span_ids, noise_step, ada_table, w_qkv, w_out):
    num_slot = lax.axis_size("slot")
    num_ctx = lax.axis_size("ctx")
    my_slot = lax.axis_index("slot")
    tok_dev = latents.shape[1]
    width = latents.shape[2]
    tokens = tok_dev * num_ctx
    heads_dev = -(-HEADS // num_ctx)
    share = HEADS // KV_GROUPS
    levels_all = ada_table.shape[0]
    slot_range = jnp.arange(num_slot, dtype=jnp.int32)
    pick_int = (slot_range == my_slot).astype(jnp.int32)
    pick_float = pick_int.astype(jnp.float32)
    out_cols = w_out.shape[1]
    block_rows = math.gcd(tokens, 512)
    num_blocks = tokens // block_rows
    scale = 1.0 / HD**0.5

    def one_step(own_latent, ids, levels):
        onehot = (levels[:, None] == jnp.arange(levels_all, dtype=jnp.int32)[None, :]).astype(
            jnp.float32
        )
        modulation = jnp.dot(
            onehot, ada_table.reshape(levels_all, 3 * width), precision=lax.Precision.HIGHEST
        )
        modulation = modulation.reshape(num_slot, 3, width)
        own_mod = jnp.einsum("s,scd->cd", pick_float, modulation, precision=lax.Precision.HIGHEST)
        own_id = jnp.sum(pick_int * ids)
        values = own_latent.astype(jnp.float32)
        center = jnp.mean(values, axis=-1, keepdims=True)
        spread = jnp.mean((values - center) ** 2, axis=-1, keepdims=True)
        normed = (values - center) * lax.rsqrt(spread + EPS)
        hidden = (normed * (1.0 + own_mod[1][None, :]) + own_mod[0][None, :]).astype(jnp.bfloat16)
        columns = jnp.dot(
            lax.all_gather(hidden, "slot", axis=0, tiled=True),
            w_qkv,
            preferred_element_type=jnp.float32,
        ).astype(jnp.bfloat16)
        qkv_own = lax.all_to_all(columns, "slot", split_axis=0, concat_axis=1, tiled=True)
        query_own = qkv_own[:, : HEADS * HD].reshape(tok_dev, 1, HEADS, HD)
        pair_own = qkv_own[:, HEADS * HD :].reshape(tok_dev, 2, KV_GROUPS, HD)
        pair_own = jnp.repeat(pair_own, share, axis=2)
        stacked = jnp.concatenate([query_own, pair_own], axis=1)
        stacked = jnp.pad(stacked, ((0, 0), (0, 0), (0, num_ctx * heads_dev - HEADS), (0, 0)))
        stacked = stacked.reshape(tok_dev, 3, num_ctx * heads_dev * HD)
        spread_rows = lax.all_to_all(stacked, "ctx", split_axis=2, concat_axis=0, tiled=True)
        query_blocks = spread_rows[:, 0].reshape(num_blocks, block_rows, heads_dev, HD)
        key_rows = spread_rows[:, 1]
        value_rows = spread_rows[:, 2]
        start_state = (
            jnp.full((num_blocks, heads_dev, block_rows), NEG, jnp.float32),
            jnp.zeros((num_blocks, heads_dev, block_rows), jnp.float32),
            jnp.zeros((num_blocks, heads_dev, block_rows, HD), jnp.float32),
        )
        key_part = lax.all_gather(key_rows, "slot", axis=0, tiled=True)
        value_part = lax.all_gather(value_rows, "slot", axis=0, tiled=True)
        count = key_part.shape[0]
        key_heads = key_part.reshape(count, heads_dev, HD)
        value_heads = value_part.reshape(count, heads_dev, HD)
        slot_of = jnp.arange(count, dtype=jnp.int32) // tokens
        key_ids = jnp.sum(
            jnp.where(slot_of[:, None] == slot_range[None, :], ids[None, :], 0), axis=1
        )
        allowed = key_ids <= own_id

        def per_block(bargs):
            query_blk, top_old, total_old, accum_old = bargs
            scores = (
                jnp.einsum("qhd,khd->hqk", query_blk, key_heads, preferred_element_type=jnp.float32)
                * scale
            )
            scores = jnp.where(allowed[None, None, :], scores, NEG)
            top_new = jnp.maximum(top_old, jnp.max(scores, axis=-1))
            weights = jnp.where(allowed[None, None, :], jnp.exp(scores - top_new[..., None]), 0.0)
            factor = jnp.exp(top_old - top_new)
            total_new = total_old * factor + jnp.sum(weights, axis=-1)
            probs = weights.astype(jnp.bfloat16)
            accum_new = accum_old * factor[..., None] + jnp.einsum(
                "hqk,khd->hqd", probs, value_heads, preferred_element_type=jnp.float32
            )
            return (top_new, total_new, accum_new)

        def compute(state):
            top_all, total_all, accum_all = state
            return lax.map(per_block, (query_blocks, top_all, total_all, accum_all))

        def keep(state):
            return state

        state = lax.cond(jnp.any(allowed), compute, keep, start_state)
        top_all, total_all, accum_all = state
        attn_heads = (accum_all / total_all[..., None]).astype(jnp.bfloat16)
        attn_heads = attn_heads.transpose(0, 2, 1, 3).reshape(tokens, heads_dev * HD)
        attn_back = lax.all_to_all(attn_heads, "ctx", split_axis=0, concat_axis=1, tiled=True)
        attn_own = attn_back[:, : HEADS * HD]
        gate_cols = lax.dynamic_slice_in_dim(modulation[:, 2], my_slot * out_cols, out_cols, 1)
        portion = lax.all_gather(attn_own, "slot", axis=0, tiled=True)
        count = portion.shape[0]
        span_of = jnp.arange(count, dtype=jnp.int32) // tok_dev
        select = (span_of[:, None] == slot_range[None, :]).astype(jnp.float32)
        gate_rows = jnp.dot(select, gate_cols, precision=lax.Precision.HIGHEST)
        product = jnp.dot(portion, w_out, preferred_element_type=jnp.float32)
        out_columns = (product * gate_rows).astype(jnp.bfloat16)
        return lax.all_to_all(out_columns, "slot", split_axis=0, concat_axis=1, tiled=True)

    rank = jnp.sum((span_ids[None, :] < span_ids[:, None]).astype(jnp.int32), axis=1)
    level_one = rank * PER + noise_step + 1
    own_latent = latents[0]
    vel_one = one_step(own_latent, span_ids, level_one)
    step_size = 1.0 / (num_slot * PER)
    moved = (own_latent.astype(jnp.float32) - vel_one.astype(jnp.float32) * step_size).astype(
        jnp.bfloat16
    )
    first = span_ids == jnp.min(span_ids)
    first_int = first.astype(jnp.int32)
    mine_first = jnp.sum(pick_int * first_int) > 0
    root_slot = jnp.sum(first_int * slot_range)
    whole = from_root(moved, "slot", root_slot)
    finished = lax.dynamic_slice_in_dim(whole, my_slot * (width // num_slot), width // num_slot, 1)
    moved = jnp.where(mine_first, fresh, moved)
    ids_two = jnp.where(first, num_slot, span_ids)
    level_two = jnp.where(first, num_slot * PER, level_one - 1)
    vel_two = one_step(moved, ids_two, level_two)
    velocity = jnp.stack([vel_one, vel_two])[:, None, :, :]
    return (velocity, finished)


def solution(mesh):
    in_specs = (
        P("slot", "ctx", None),
        P("ctx", None),
        P(),
        P(),
        P(),
        P(None, "slot"),
        P(None, "slot"),
    )
    out_specs = (P(None, "slot", "ctx", None), P("ctx", "slot"))
    return jax.shard_map(shards, mesh=mesh, in_specs=in_specs, out_specs=out_specs, check_vma=False)
```

profile of v0, /device:TPU:1, one launch (start us, length us, event | category | flops | bytes accessed | tf_op | source)
XLA Modules:
  0.0 605.8 jit_solution(4298946823310025938)
XLA Ops:
  17.7 27.4 %all-gather.13.cloned.1.call-done = bf16[256,3072]{1,0:T(8,128)(2,1)} async-done(((bf16[64,3072]{1,0:T(8,128)(2,1)}), bf16[256,3072]{1,0:T(8,128)(2,1)}) %all-gather.13.cloned.1.call-update) | async-done | bytes 1572880 | tf_op jit(solution)/shard_map/all_gather | solution.py:57
  45.1 5.9 convolution_convert_fusion.1
  51.1 13.4 %all_to_all.144 = bf16[4,64,1280]{2,1,0:T(8,128)(2,1)S(1)} all-to-all(bf16[4,64,1280]{2,1,0:T(8,128)(2,1)S(1)} %bitcast.260), channel_id=1, replica_groups=mesh['slot'=4,'ctx'=32] {'slot'}, dimensions={0} | all-to-all | bytes 1310720 | tf_op jit(solution)/shard_map/all_to_all | solution.py:61
  74.8 6.1 %reshape.326 = bf16[32,2,12288]{2,1,0:T(2,128)(2,1)S(1)} reshape(bf16[4096,3,64]{2,1,0:T(4,128)(2,1)} %bitcast.231) | data formatting | bytes 3145728
  80.9 27.7 %all_to_all.145 = bf16[32,2,12288]{2,1,0:T(2,128)(2,1)S(1)} all-to-all(bf16[32,2,12288]{2,1,0:T(2,128)(2,1)S(1)} %reshape.326), channel_id=1, replica_groups=mesh['slot'=4,'ctx'=32] {'ctx'}, dimensions={0} | all-to-all | bytes 3145728 | tf_op jit(solution)/shard_map/all_to_all | solution.py:68
  123.8 22.1 %all-gather.23.cloned.1.call-done = bf16[8192,1,128]{2,0,1:T(8,128)(2,1)} async-done(((bf16[2048,1,128]{2,0,1:T(8,128)(2,1)}), bf16[8192,1,128]{2,0,1:T(8,128)(2,1)}) %all-gather.23.cloned.1.call-update) | async-done | bytes 2097168 | tf_op jit(solution)/shard_map/all_gather | solution.py:78
  145.9 27.8 %all-gather.21.cloned.1.call-done = bf16[8192,1,128]{2,0,1:T(8,128)(2,1)} async-done(((bf16[2048,1,128]{2,0,1:T(8,128)(2,1)}), bf16[8192,1,128]{2,0,1:T(8,128)(2,1)}) %all-gather.21.cloned.1.call-update) | async-done | bytes 2097168 | tf_op jit(solution)/shard_map/all_gather | solution.py:77
  173.7 60.3 %conditional.2 = (f32[4,1,512]{2,1,0:T(1,128)}, f32[4,1,512,128]{3,2,1,0:T(8,128)}) conditional(s32[]{:T(128)} %convert_element_type.72, () %tuple.32, (bf16[2048,3,128]{2,0,1:T(8,128)(2,1)S(1)}, bf16[8192,128]{1,0:T(8,128)(2,1)}, bf16[8192,128]{1,0:T(8,128)(2,1)}, pred[8192]{0:T(1024)(128)(4,1)S(1)}) %tuple.126), branch_computations={%region_6.7_spmd, %region_7.12_spmd} | conditional | flops 2202076672 | bytes 64407772 | solution.py:112
  173.8 60.2 %while.22 = (s32[]{:T(128)}, f32[4,1,512]{2,1,0:T(1,128)}, f32[4,1,512,128]{3,2,1,0:T(8,128)}, pred[8192]{0:T(1024)(128)(4,1)S(1)}, bf16[4,512,1,128]{3,1,2,0:T(...) while((s32[]{:T(128)}, f32[4,1,512]{2,1,0:T(1,128)}, ...), condition=%wide.region_11.11_spmd, body=%wide.region_8.10_spmd.sunk | while | flops 2202076672 | bytes 63359108 | solution.py:107
  236.3 17.0 %all_to_all.146 = bf16[32,64,128]{2,1,0:T(8,128)(2,1)S(1)} all-to-all(bf16[32,64,128]{2,1,0:T(8,128)(2,1)S(1)} %bitcast.253), channel_id=1, replica_groups=mesh['slot'=4,'ctx'=32] {'ctx'}, dimensions={0} | all-to-all | bytes 1048576 | tf_op jit(solution)/shard_map/all_to_all | solution.py:116
  255.2 21.7 %all-gather.15.cloned.1.call-done = bf16[256,3072]{1,0:T(8,128)(2,1)} async-done(((bf16[64,3072]{1,0:T(8,128)(2,1)}), bf16[256,3072]{1,0:T(8,128)(2,1)}) %all-gather.15.cloned.1.call-update) | async-done | bytes 1572880 | tf_op jit(solution)/shard_map/all_gather | solution.py:119
  286.6 7.5 %all-to-all-done.3 = bf16[4,64,768]{2,1,0:T(8,128)(2,1)S(1)} async-done(((bf16[4,64,768]{2,1,0:T(8,128)(2,1)}), bf16[4,64,768]{2,1,0:T(8,128)(2,1)S(1)}, u32[]{:S(2)}, u32[]{:S(2)}) %all-to-all-start.3) | async-done | bytes 393248 | tf_op jit(solution)/shard_map/all_to_all | solution.py:126
  296.8 23.2 %all-gather.17.cloned.1.call-done = bf16[256,3072]{1,0:T(8,128)(2,1)} async-done(((bf16[64,3072]{1,0:T(8,128)(2,1)}), bf16[256,3072]{1,0:T(8,128)(2,1)}) %all-gather.17.cloned.1.call-update) | async-done | bytes 1572880 | tf_op jit(solution)/shard_map/all_gather | solution.py:57
  320.0 5.9 convolution_convert_fusion
  325.9 13.4 %all_to_all.147 = bf16[4,64,1280]{2,1,0:T(8,128)(2,1)S(1)} all-to-all(bf16[4,64,1280]{2,1,0:T(8,128)(2,1)S(1)} %bitcast.261), channel_id=1, replica_groups=mesh['slot'=4,'ctx'=32] {'slot'}, dimensions={0} | all-to-all | bytes 1310720 | tf_op jit(solution)/shard_map/all_to_all | solution.py:61
  349.6 6.1 %reshape.328 = bf16[32,2,12288]{2,1,0:T(2,128)(2,1)S(1)} reshape(bf16[4096,3,64]{2,1,0:T(4,128)(2,1)} %bitcast.230) | data formatting | bytes 3145728
  355.7 27.7 %all_to_all.148 = bf16[32,2,12288]{2,1,0:T(2,128)(2,1)S(1)} all-to-all(bf16[32,2,12288]{2,1,0:T(2,128)(2,1)S(1)} %reshape.328), channel_id=1, replica_groups=mesh['slot'=4,'ctx'=32] {'ctx'}, dimensions={0} | all-to-all | bytes 3145728 | tf_op jit(solution)/shard_map/all_to_all | solution.py:68
  397.7 22.9 %all-gather.27.cloned.1.call-done = bf16[8192,1,128]{2,0,1:T(8,128)(2,1)} async-done(((bf16[2048,1,128]{2,0,1:T(8,128)(2,1)}), bf16[8192,1,128]{2,0,1:T(8,128)(2,1)}) %all-gather.27.cloned.1.call-update) | async-done | bytes 2097168 | tf_op jit(solution)/shard_map/all_gather | solution.py:78
  420.6 27.8 %all-gather.25.cloned.1.call-done = bf16[8192,1,128]{2,0,1:T(8,128)(2,1)} async-done(((bf16[2048,1,128]{2,0,1:T(8,128)(2,1)}), bf16[8192,1,128]{2,0,1:T(8,128)(2,1)}) %all-gather.25.cloned.1.call-update) | async-done | bytes 2097168 | tf_op jit(solution)/shard_map/all_gather | solution.py:77
  448.4 60.3 %conditional.3 = (f32[4,1,512]{2,1,0:T(1,128)}, f32[4,1,512,128]{3,2,1,0:T(8,128)}) conditional(s32[]{:T(128)} %convert_element_type.82, () %tuple.34, (bf16[2048,3,128]{2,0,1:T(8,128)(2,1)S(1)}, bf16[8192,128]{1,0:T(8,128)(2,1)}, bf16[8192,128]{1,0:T(8,128)(2,1)}, pred[8192]{0:T(1024)(128)(4,1)S(1)}) %tuple.128), branch_computations={%region_19.20_spmd, %region_20.25_spmd} | conditional | flops 2202076672 | bytes 64407772 | solution.py:112
  448.4 60.2 %while.23 = (s32[]{:T(128)}, f32[4,1,512]{2,1,0:T(1,128)}, f32[4,1,512,128]{3,2,1,0:T(8,128)}, pred[8192]{0:T(1024)(128)(4,1)S(1)}, bf16[4,512,1,128]{3,1,2,0:T(...) while((s32[]{:T(128)}, f32[4,1,512]{2,1,0:T(1,128)}, ...), condition=%wide.region_24.24_spmd, body=%wide.region_21.23_spmd.sunk | while | flops 2202076672 | bytes 63359108 | solution.py:107
  511.0 17.0 %all_to_all.149 = bf16[32,64,128]{2,1,0:T(8,128)(2,1)S(1)} all-to-all(bf16[32,64,128]{2,1,0:T(8,128)(2,1)S(1)} %bitcast.254), channel_id=1, replica_groups=mesh['slot'=4,'ctx'=32] {'ctx'}, dimensions={0} | all-to-all | bytes 1048576 | tf_op jit(solution)/shard_map/all_to_all | solution.py:116
  530.8 20.8 %all-gather.19.cloned.1.call-done = bf16[256,3072]{1,0:T(8,128)(2,1)} async-done(((bf16[64,3072]{1,0:T(8,128)(2,1)}), bf16[256,3072]{1,0:T(8,128)(2,1)}) %all-gather.19.cloned.1.call-update) | async-done | bytes 1572880 | tf_op jit(solution)/shard_map/all_gather | solution.py:119
  561.3 34.9 %all-reduce.4.cloned.1.call-done = bf16[64,3072]{1,0:T(8,128)(2,1)} async-done(((bf16[64,3072]{1,0:T(8,128)(2,1)}), bf16[64,3072]{1,0:T(8,128)(2,1)}) %all-reduce.4.cloned.1.call-update) | async-done | bytes 393232 | tf_op jit(solution)/shard_map/psum | solution.py:20
  (197 shorter events, 212.3 us)
Async XLA Ops:
  7.2 9.5 %copy-start = (bf16[1,64,3072]{2,1,0:T(8,128)(2,1)S(1)}, bf16[1,64,3072]{2,1,0:T(8,128)(2,1)}, u32[]{:S(2)}) copy-start(bf16[1,64,3072]{2,1,0:T(8,128)(2,1)} %param.15) | copy-start | bytes 1179652
  7.2 37.9 %all-gather.13.cloned.1.call-start = ((), (), s32[]{:S(2)}) async-start(), calls=%async_computation.8 | async-start | bytes 1966080 | tf_op jit(solution)/shard_map/all_gather | solution.py:57
  13.6 37.4 %copy-start.3 = (f32[3,3072,9]{1,0,2:T(4,128)}, f32[3,3072,9]{1,0,2:T(4,128)S(1)}, u32[]{:S(2)}) copy-start(f32[3,3072,9]{1,0,2:T(4,128)S(1)} %dot_general.47) | copy-start | bytes 995332
  16.3 34.8 %copy-start.8 = (f32[4,3,3072]{2,0,1:T(4,128)}, f32[4,3,3072]{2,0,1:T(4,128)S(1)}, u32[]{:S(2)}) copy-start(f32[4,3,3072]{2,0,1:T(4,128)S(1)} %fusion.81) | copy-start | bytes 442372
  17.7 128.3 %all-gather.23.cloned.1.call-start = ((), (), s32[]{:S(2)}) async-start(), calls=%async_computation.14 | async-start | bytes 2621440 | tf_op jit(solution)/shard_map/all_gather | solution.py:78
  113.3 7.7 %copy-start.11 = (s32[4]{0:T(128)S(1)}, s32[4]{0:T(128)}, u32[]{:S(2)}) copy-start(s32[4]{0:T(128)} %param.17) | copy-start | bytes 52
  120.2 53.5 %all-gather.21.cloned.1.call-start = ((), (), s32[]{:S(2)}) async-start(), calls=%async_computation.13 | async-start | bytes 2621440 | tf_op jit(solution)/shard_map/all_gather | solution.py:77
  120.9 155.9 %all-gather.15.cloned.1.call-start = ((), (), s32[]{:S(2)}) async-start(), calls=%async_computation.9 | async-start | bytes 1966080 | tf_op jit(solution)/shard_map/all_gather | solution.py:119
  234.0 20.2 %copy-start.4 = (f32[3,3072,9]{1,0,2:T(4,128)S(1)}, f32[3,3072,9]{1,0,2:T(4,128)}, u32[]{:S(2)}) copy-start(f32[3,3072,9]{1,0,2:T(4,128)} %copy-done.3) | copy-start | bytes 995332
  254.2 26.8 %slice-start.1 = ((f32[4,3,3072]{2,0,1:T(4,128)}), f32[4,1,3072]{2,0,1:T(4,128)S(1)}, s32[]{:S(2)}) async-start(f32[4,3,3072]{2,0,1:T(4,128)} %copy-done.8), calls=%async_computation.18 | async-start | bytes 98304 | tf_op jit(solution)/shard_map/slice | solution.py:118
  254.7 27.6 %copy-start.7 = (f32[4,3,3072]{2,0,1:T(4,128)}, f32[4,3,3072]{2,0,1:T(4,128)S(1)}, u32[]{:S(2)}) copy-start(f32[4,3,3072]{2,0,1:T(4,128)S(1)} %fusion.79) | copy-start | bytes 442372
  255.2 40.0 %copy-start.9 = (bf16[64,3072]{1,0:T(8,128)(2,1)S(1)}, bf16[64,3072]{1,0:T(8,128)(2,1)}, u32[]{:S(2)}) copy-start(bf16[64,3072]{1,0:T(8,128)(2,1)} %param.16) | copy-start | bytes 1179652
  282.3 11.8 %all-to-all-start.3 = ((bf16[4,64,768]{2,1,0:T(8,128)(2,1)}), bf16[4,64,768]{2,1,0:T(8,128)(2,1)S(1)}, u32[]{:S(2)}, u32[]{:S(2)}) async-start(bf16[4,64,768]{2,1,0:T(8,128)(2,1)} %bitcast.39), calls=%async_computation.3 | async-start | bytes 786432 | tf_op jit(solution)/shard_map/all_to_all | solution.py:126
  286.0 33.9 %all-gather.17.cloned.1.call-start = ((), (), s32[]{:S(2)}) async-start(), calls=%async_computation.10 | async-start | bytes 1966080 | tf_op jit(solution)/shard_map/all_gather | solution.py:57
  294.1 31.8 %copy-start.5 = (bf16[4,64,768]{2,1,0:T(8,128)(2,1)}, bf16[4,64,768]{2,1,0:T(8,128)(2,1)S(1)}, u32[]{:S(2)}) copy-start(bf16[4,64,768]{2,1,0:T(8,128)(2,1)S(1)} %all-to-all-done.3) | copy-start | bytes 1179652
  296.7 123.9 %all-gather.27.cloned.1.call-start = ((), (), s32[]{:S(2)}) async-start(), calls=%async_computation.16 | async-start | bytes 2621440 | tf_op jit(solution)/shard_map/all_gather | solution.py:78
  388.1 7.7 %copy-start.10 = (s32[8192]{0:T(1024)S(1)}, s32[8192]{0:T(1024)}, u32[]{:S(2)}) copy-start(s32[8192]{0:T(1024)} %get-tuple-element.175) | copy-start | bytes 98308
  395.0 53.3 %all-gather.25.cloned.1.call-start = ((), (), s32[]{:S(2)}) async-start(), calls=%async_computation.15 | async-start | bytes 2621440 | tf_op jit(solution)/shard_map/all_gather | solution.py:77
  395.8 155.7 %all-gather.19.cloned.1.call-start = ((), (), s32[]{:S(2)}) async-start(), calls=%async_computation.11 | async-start | bytes 1966080 | tf_op jit(solution)/shard_map/all_gather | solution.py:119
  508.6 21.3 %copy-start.2 = (f32[4,8,8,768]{3,2,0,1:T(8,128)S(1)}, f32[4,8,8,768]{3,2,0,1:T(8,128)}, u32[]{:S(2)}) copy-start(f32[4,8,8,768]{3,2,0,1:T(8,128)} %copy-done.1) | copy-start | bytes 2359300
  528.9 67.3 %all-reduce.4.cloned.1.call-start = ((), (), s32[]{:S(2)}) async-start(), calls=%async_computation.12 | async-start | bytes 786432 | tf_op jit(solution)/shard_map/psum | solution.py:20
  530.7 25.0 %slice-start = ((f32[4,3,3072]{2,0,1:T(4,128)}), f32[4,1,3072]{2,0,1:T(4,128)S(1)}, s32[]{:S(2)}) async-start(f32[4,3,3072]{2,0,1:T(4,128)} %copy-done.7), calls=%async_computation.17 | async-start | bytes 98304 | tf_op jit(solution)/shard_map/slice | solution.py:118
  530.8 30.0 %copy-start.6 = (bf16[4,64,768]{2,1,0:T(8,128)(2,1)S(1)}, bf16[4,64,768]{2,1,0:T(8,128)(2,1)}, u32[]{:S(2)}) copy-start(bf16[4,64,768]{2,1,0:T(8,128)(2,1)} %copy-done.5) | copy-start | bytes 1179652
  557.0 40.7 %all-to-all-start.7 = ((bf16[4,64,768]{2,1,0:T(8,128)(2,1)}), bf16[4,64,768]{2,1,0:T(8,128)(2,1)S(1)}, u32[]{:S(2)}, u32[]{:S(2)}) async-start(bf16[4,64,768]{2,1,0:T(8,128)(2,1)} %bitcast.60), calls=%async_computation.7 | async-start | bytes 786432 | tf_op jit(solution)/shard_map/all_to_all | solution.py:126
  (9 other events, 42.7 us)
Sparse Core Ops, SparseCore 0:
  17.8 27.2 all-gather.12
  120.3 25.5 all-gather.22
  147.6 26.0 all-gather.20
  254.3 22.4 all-gather.14
  296.8 23.1 all-gather.16
  395.1 25.4 all-gather.26
  422.3 26.0 all-gather.24
  529.0 22.4 all-gather.18
  554.0 42.1 all-reduce.3
where the time goes:
time: 607 us; the launch traced here: 606 us
  waiting for transfers between devices  237 us (39%)
  blocking collectives  116 us (19%)
  matrix products  98.3 us (16%)
  local copies, waits for them, and re-layouts  67.1 us (11%)
  other arithmetic  61.5 us (10%)
  between operations  17 us (3%)
  starting transfers between devices  7.99 us (1%)
    all_gather x2, waiting for transfers between devices, one_step(): key_part = lax.all_gather(key_rows, 'slot', axis=0, tiled=True)  55.5 us
    all_to_all x2, blocking collectives, one_step(): lax.all_to_all(stacked, 'ctx', split_axis=2, concat_axis=0, tiled=True)  55.3 us
    all_gather x2, waiting for transfers between devices, one_step(): lax.all_gather(hidden, 'slot', axis=0, tiled=True)  50.6 us
    all_gather x2, waiting for transfers between devices, one_step(): value_part = lax.all_gather(value_rows, 'slot', axis=0, tiled=True)  45 us
    all_gather x2, waiting for transfers between devices, one_step(): portion = lax.all_gather(attn_own, 'slot', axis=0, tiled=True)  42.4 us
    reduce_sum x8, other arithmetic, per_block(): total_new = total_old * factor + jnp.sum(weights, axis=-1)  41.6 us
    dot_general x8, matrix products, per_block(): jnp.einsum('hqk,khd->hqd', probs, value_heads, preferred_element_type=jnp...  40.3 us
    unnamed x42, local copies, waits for them, and re-layouts  35.1 us
  transfers between devices with their start and end apart: 11, of which 10 were waited for; matrix products, arithmetic and copies ran while one was open for 2% of the time, Pallas kernels for 0%

commit v1 on v0

v1 whole, which is shorter than its diff:
```python
import math

import jax
import jax.numpy as jnp
from jax import lax
from jax.experimental import pallas as pl
from jax.experimental.pallas import tpu as pltpu
from jax.sharding import PartitionSpec as P

HD = 128
EPS = 1e-06
BF = jnp.bfloat16
F32 = jnp.float32
AXES = ("slot", "ctx")
VM = pl.BlockSpec(memory_space=pltpu.VMEM)
SM = pl.BlockSpec(memory_space=pltpu.SMEM)
SLOTS = 4
PER = 2
TOK = 64
HALF = 32
ROWS = SLOTS * HALF
WIDTH = 3072
COLS = WIDTH // SLOTS
LOG2E = 1.4426950408889634


def where_is(flat):
    s, c = flat // 32, flat % 32
    return dict(h=s // 2, i=s % 2, z=c // 8, xl=(c // 4) % 2, y=c % 4)


def flat_of(d):
    return (d["h"] * 2 + d["i"]) * 32 + d["z"] * 8 + d["xl"] * 4 + d["y"]


def move(x, h=0, i=0, z=0, y=0):
    pairs = []
    for f in range(128):
        d = where_is(f)
        d["h"] = (d["h"] + h) % 2
        d["i"] = (d["i"] + i) % 2
        d["z"] = (d["z"] + z) % 4
        d["y"] = (d["y"] + y) % 4
        pairs.append((f, flat_of(d)))
    return lax.ppermute(x, AXES, pairs)


def group_lists():
    out = []
    for i in range(2):
        for z in range(4):
            for yh in range(2):
                out.append(
                    [
                        flat_of(dict(h=h, i=i, z=z, xl=xl, y=2 * yh + yl))
                        for h in range(2)
                        for xl in range(2)
                        for yl in range(2)
                    ]
                )
    return out


def exchange(x):
    return lax.all_to_all(x, AXES, 0, 0, tiled=True, axis_index_groups=group_lists())


def params(mib, **kw):
    return pltpu.CompilerParams(vmem_limit_bytes=mib * 1024 * 1024, **kw)


def first_slot(ids):
    best, at = ids[0], jnp.int32(0)
    for j in range(1, SLOTS):
        less = ids[j] < best
        best = jnp.where(less, ids[j], best)
        at = jnp.where(less, j, at)
    return at


def level_of(ids, noise, t, step):
    mine = ids[t]
    rank = jnp.int32(0)
    for j in range(SLOTS):
        rank = rank + (ids[j] < mine).astype(jnp.int32)
    level = PER * rank + noise[t] + 1
    if step == 0:
        return level
    return jnp.where(rank == 0, SLOTS * PER, level - 1)


def row_of(half, slot):
    return pl.ds(pl.multiple_of((half * SLOTS + slot) * HALF, HALF), HALF)


def col_of(slot, width=COLS):
    return pl.ds(pl.multiple_of(slot * width, 128), width)


def modulated(values, ada, level):
    center = jnp.mean(values, axis=-1, keepdims=True)
    off = values - center
    spread = jnp.mean(off * off, axis=-1, keepdims=True)
    normed = off * lax.rsqrt(spread + EPS)
    return (normed * (1.0 + ada[level, 1:2, :]) + ada[level, 0:1, :]).astype(BF)


def project(hidden, w, mine, theirs):
    out = jnp.dot(hidden[...], w[...], preferred_element_type=F32).astype(BF)
    for k in range(2):
        mine[k] = out[:ROWS, k * HD : (k + 1) * HD]
        theirs[k] = out[ROWS:, k * HD : (k + 1) * HD]


def first_body(pos, ids, noise, x0, x1, x2, x3, ada, w, mine, theirs, hidden):
    s = pos[0]
    i = s % 2

    @pl.when(pl.program_id(0) == 0)
    def _():
        for r, x in enumerate((x0, x1, x2, x3)):
            t = s ^ r
            level = level_of(ids, noise, t, 0)
            for a in range(2):
                values = x[a * HALF : (a + 1) * HALF, :].astype(F32)
                hidden[row_of(i ^ a, t), :] = modulated(values, ada, level)

    project(hidden, w, mine, theirs)


def second_body(
    pos, ids, noise, x0, x1, x2, x3, v0, v1, v2, v3, fresh, ada, w,
    mine, theirs, vel, fin, hidden, vall, moved,
):
    s = pos[0]
    i = s % 2

    @pl.when(pl.program_id(0) == 0)
    def _():
        for k, v in enumerate((v0, v1, v2, v3)):
            if k % 2 == 0:
                vall[:, col_of(s ^ k)] = v[...]
            else:
                vall[:ROWS, col_of(s ^ k)] = v[ROWS:, :]
                vall[ROWS:, col_of(s ^ k)] = v[:ROWS, :]
        first = first_slot(ids)
        for a in range(2):
            vel[a * HALF : (a + 1) * HALF, :] = vall[row_of(i ^ a, s), :]
        for r, x in enumerate((x0, x1, x2, x3)):
            t = s ^ r
            level = level_of(ids, noise, t, 1)
            for a in range(2):
                rows = slice(a * HALF, (a + 1) * HALF)
                where = row_of(i ^ a, t)
                moved[...] = (
                    x[rows, :].astype(F32) - vall[where, :].astype(F32) * (1.0 / (SLOTS * PER))
                ).astype(BF)

                @pl.when(t == first)
                def _():
                    fin[rows, :] = moved[:, col_of(s)]
                    moved[...] = fresh[rows, :]

                hidden[where, :] = modulated(moved[...].astype(F32), ada, level)

    project(hidden, w, mine, theirs)


def whole(shape):
    return pl.BlockSpec(shape, lambda n: (0,) * len(shape))


def projected_shapes(heads):
    return [jax.ShapeDtypeStruct((heads, ROWS, HD), BF)] * 2


def first_projection(pos, ids, noise, xs, ada, w):
    heads = w.shape[1] // HD
    return pl.pallas_call(
        first_body,
        grid=(heads // 2,),
        in_specs=[SM, SM, SM]
        + [whole((TOK, WIDTH))] * 4
        + [whole(ada.shape), pl.BlockSpec((WIDTH, 2 * HD), lambda n: (0, n))],
        out_specs=[pl.BlockSpec((2, ROWS, HD), lambda n: (n, 0, 0))] * 2,
        out_shape=projected_shapes(heads),
        scratch_shapes=[pltpu.VMEM((2 * ROWS, WIDTH), BF)],
        compiler_params=params(32),
        name="modulate_project",
    )(pos, ids, noise, *xs, ada, w)


def second_projection(pos, ids, noise, xs, vs, fresh, ada, w):
    heads = w.shape[1] // HD
    return pl.pallas_call(
        second_body,
        grid=(heads // 2,),
        in_specs=[SM, SM, SM]
        + [whole((TOK, WIDTH))] * 4
        + [whole((2 * ROWS, COLS))] * 4
        + [whole((TOK, WIDTH)), whole(ada.shape), pl.BlockSpec((WIDTH, 2 * HD), lambda n: (0, n))],
        out_specs=[pl.BlockSpec((2, ROWS, HD), lambda n: (n, 0, 0))] * 2
        + [whole((TOK, WIDTH)), whole((TOK, COLS))],
        out_shape=projected_shapes(heads)
        + [jax.ShapeDtypeStruct((TOK, WIDTH), BF), jax.ShapeDtypeStruct((TOK, COLS), BF)],
        scratch_shapes=[
            pltpu.VMEM((2 * ROWS, WIDTH), BF),
            pltpu.VMEM((2 * ROWS, WIDTH), BF),
            pltpu.VMEM((HALF, WIDTH), BF),
        ],
        compiler_params=params(40),
        name="advance_modulate_project",
    )(pos, ids, noise, *xs, *vs, fresh, ada, w)


def pack_body(pos, mine, other, kv, q, chip):
    i, h = pos[0] % 2, pos[0] // 2
    chip[pl.ds(10 * i, 10)] = mine[...]
    chip[pl.ds(10 * (1 - i), 10)] = other[...]
    for g in range(8):
        kv[g, 0] = chip[4 + g]
        kv[g, 1] = chip[12 + g]

    @pl.when(h == 0)
    def _():
        q[0:20] = chip[...]
        q[20:24] = jnp.zeros((4, ROWS, HD), BF)

    @pl.when(h != 0)
    def _():
        q[0:20] = jnp.zeros((20, ROWS, HD), BF)
        q[20:24] = chip[0:4]


def pack(pos, mine, other):
    return pl.pallas_call(
        pack_body,
        in_specs=[SM, VM, VM],
        out_specs=[VM, VM],
        out_shape=[
            jax.ShapeDtypeStruct((8, 2, ROWS, HD), BF),
            jax.ShapeDtypeStruct((24, ROWS, HD), BF),
        ],
        scratch_shapes=[pltpu.VMEM((20, ROWS, HD), BF)],
        compiler_params=params(16),
        name="pack_heads",
    )(pos, mine, other)


NB = 64
KEYS = NB * HALF
QROWS = 4 * 3 * HALF


def attend_body(step, parts, ids, q, *refs):
    blocks = refs[:parts]
    out, qs, ks, vs, top, acc = refs[parts:]
    at = 0
    for ref in blocks:
        for b in range(ref.shape[0]):
            for j in range(SLOTS):
                rows = slice(j * HALF, (j + 1) * HALF)
                ks[j, at * HALF : (at + 1) * HALF, :] = ref[b, 0, rows, :]
                vs[j, at * HALF : (at + 1) * HALF, :HD] = ref[b, 1, rows, :]
            at += 1
    vs[:, :, HD:] = jnp.ones((SLOTS, KEYS, HD), BF)
    for c in range(4):
        for m in range(3):
            both = q[c, m] + q[4 + c, m]
            for j in range(SLOTS):
                qs[j, (c * 3 + m) * HALF : (c * 3 + m + 1) * HALF, :] = both[j * HALF : (j + 1) * HALF]
    factor = LOG2E / math.sqrt(HD)

    def id_of(t):
        if step == 0:
            return ids[t]
        return jnp.where(first_slot(ids) == t, SLOTS, ids[t])

    def per_span(t, _):
        top[...] = jnp.full_like(top, -1e30)
        acc[...] = jnp.zeros_like(acc)
        own = id_of(t)

        def per_key(j, _):
            @pl.when(id_of(j) <= own)
            def _():
                for n in range(0, KEYS, 1024):
                    scores = lax.dot_general(
                        qs[t], ks[j, n : n + 1024, :], (((1,), (1,)), ((), ())), preferred_element_type=F32
                    )
                    old = top[...]
                    new = jnp.maximum(old, jnp.max(scores, axis=-1, keepdims=True))
                    weights = jnp.exp2((scores - new) * factor).astype(BF)
                    acc[...] = acc[...] * jnp.exp2((old - new) * factor) + jnp.dot(
                        weights, vs[j, n : n + 1024, :], preferred_element_type=F32
                    )
                    top[...] = new

            return 0

        lax.fori_loop(0, SLOTS, per_key, 0)
        res = (acc[:, :HD] / acc[:, HD : HD + 1]).astype(BF)
        rows = pl.ds(pl.multiple_of(t * HALF, HALF), HALF)
        for c in range(4):
            for m in range(3):
                piece = res[(c * 3 + m) * HALF : (c * 3 + m + 1) * HALF]
                out[c, m, rows, :] = piece
                out[4 + c, m, rows, :] = piece
        return 0

    lax.fori_loop(0, SLOTS, per_span, 0)


def attend(step, ids, q, blocks):
    def body(*refs):
        attend_body(step, len(blocks), *refs)

    return pl.pallas_call(
        body,
        in_specs=[SM] + [VM] * (1 + len(blocks)),
        out_specs=VM,
        out_shape=jax.ShapeDtypeStruct((8, 3, ROWS, HD), BF),
        scratch_shapes=[
            pltpu.VMEM((SLOTS, QROWS, HD), BF),
            pltpu.VMEM((SLOTS, KEYS, HD), BF),
            pltpu.VMEM((SLOTS, KEYS, 2 * HD), BF),
            pltpu.VMEM((QROWS, 1), F32),
            pltpu.VMEM((QROWS, 2 * HD), F32),
        ],
        compiler_params=params(48),
        name="span_attention",
    )(ids, q, *blocks)


def out_body(step, pos, ids, noise, mine, other, ada, w, out, attn):
    n = pl.program_id(0)
    s = pos[0]
    i = s % 2
    width = w.shape[1]

    @pl.when(n == 0)
    def _():
        for m in range(24):
            attn[:ROWS, m * HD : (m + 1) * HD] = mine[m]
            attn[ROWS:, m * HD : (m + 1) * HD] = other[m]

    product = jnp.dot(attn[...], w[...], preferred_element_type=F32)
    cols = pl.ds(pl.multiple_of(s * COLS + n * width, 128), width)
    for t in range(SLOTS):
        gate = ada[level_of(ids, noise, t, step), 2:3, cols]
        for a in range(2):
            at = (a * SLOTS + t) * HALF
            piece = (product[at : at + HALF] * gate).astype(BF)
            if step == 0:
                out[at : at + HALF, :] = piece
            else:
                rows = pl.ds(pl.multiple_of((i ^ a) * HALF, HALF), HALF)
                out[s ^ t, rows, :] = piece


def out_projection(step, pos, ids, noise, mine, other, ada, w):
    width = 256
    if step == 0:
        out_spec = pl.BlockSpec((2 * ROWS, width), lambda n: (0, n))
        out_shape = jax.ShapeDtypeStruct((2 * ROWS, COLS), BF)
    else:
        out_spec = pl.BlockSpec((SLOTS, TOK, width), lambda n: (0, 0, n))
        out_shape = jax.ShapeDtypeStruct((SLOTS, TOK, COLS), BF)

    def body(*refs):
        out_body(step, *refs)

    return pl.pallas_call(
        body,
        grid=(COLS // width,),
        in_specs=[SM, SM, SM]
        + [whole((24, ROWS, HD))] * 2
        + [whole(ada.shape), pl.BlockSpec((WIDTH, width), lambda n: (0, n))],
        out_specs=out_spec,
        out_shape=out_shape,
        scratch_shapes=[pltpu.VMEM((2 * ROWS, WIDTH), BF)],
        compiler_params=params(32),
        name="out_projection",
    )(pos, ids, noise, mine, other, ada, w)


def finish_body(pos, vel, r0, r1, r2, r3, out):
    s = pos[0]
    out[0] = vel[...]
    for k, r in enumerate((r0, r1, r2, r3)):
        out[1, :, col_of(s ^ k)] = r[...]


def finish(pos, vel, rs):
    return pl.pallas_call(
        finish_body,
        in_specs=[SM] + [VM] * 5,
        out_specs=VM,
        out_shape=jax.ShapeDtypeStruct((2, TOK, WIDTH), BF),
        compiler_params=params(16),
        name="collect_velocity",
    )(pos, vel, *rs)


def gather_slots(x):
    far = move(x, h=1)
    near = move(x, i=1)
    return x, near, far, move(far, i=1)


def gather_keys(x):
    low, high = x[:2], x[2:]
    low_y = move(low, y=2)
    high_z = [move(high, z=k) for k in (1, -1, 2)]
    early = jnp.concatenate([x, low_y, *high_z])
    lows = jnp.concatenate([low, low_y])
    highs = jnp.concatenate([high, *high_z])
    late = [move(lows, z=k) for k in (1, -1, 2)] + [move(highs, y=2)]
    late = jnp.concatenate(late)
    return [early, move(early, i=1), late, move(late, i=1)]


def shards(latents, fresh, span_ids, noise_step, ada_table, w_qkv, w_out):
    pos = lax.axis_index("slot").astype(jnp.int32).reshape(1)
    scalars = (pos, span_ids, noise_step)
    xs = gather_slots(latents[0])

    def one_step(step, mine, theirs):
        kv, q = pack(pos, mine, move(theirs, i=1))
        keys = gather_keys(exchange(kv)[4:])
        q = exchange(q.reshape(8, 3, ROWS, HD))
        attn = exchange(attend(step, span_ids, q, keys)).reshape(24, ROWS, HD)
        return out_projection(step, *scalars, attn, move(attn, i=1), ada_table, w_out)

    vel = one_step(0, *first_projection(*scalars, xs, ada_table, w_qkv))
    mine, theirs, vel, fin = second_projection(
        *scalars, xs, gather_slots(vel), fresh, ada_table, w_qkv
    )
    out = one_step(1, mine, theirs)
    rs = [out[0], move(out[1], i=1), move(out[2], h=1), move(out[3], h=1, i=1)]
    return finish(pos, vel, rs)[:, None], fin


def solution(mesh):
    in_specs = (
        P("slot", "ctx", None),
        P("ctx", None),
        P(),
        P(),
        P(),
        P(None, "slot"),
        P(None, "slot"),
    )
    out_specs = (P(None, "slot", "ctx", None), P("ctx", "slot"))
    return jax.shard_map(shards, mesh=mesh, in_specs=in_specs, out_specs=out_specs, check_vma=False)
```

time: 607 us -> 261 us (0.43)
  waiting for transfers between devices: 237 us -> 56.1 us
  matrix products: 98.3 us -> 0 us
  other arithmetic: 61.5 us -> 0.19 us
  Pallas kernels: 0 us -> 59.6 us
  local copies, waits for them, and re-layouts: 67.1 us -> 9.52 us
  starting transfers between devices: 7.99 us -> 49.9 us
  blocking collectives: 116 us -> 84.4 us
  between operations: 17 us -> 0.95 us
    all_gather x8 -> x0, waiting for transfers between devices: 194 us -> none  [the longest x2 55.5 us: one_step(): key_part = lax.all_gather(key_rows, 'slot', axis=0, tiled=True)]
    dot_general x26 -> x0, matrix products: 98.3 us -> none  [the longest x8 40.3 us: per_block(): jnp.einsum('hqk,khd->hqd', probs, value_heads, preferred_element_type=jnp...]
    pallas_call x0 -> x9, Pallas kernels: none -> 59.6 us  [the longest x2 39.9 us: attend(): pl.pallas_call(body, in_specs=[SM] + [VM] * (1 + len(blocks)), out_specs=...]
    ppermute x0 -> x33, waiting for transfers between devices: none -> 56.1 us  [move(): return lax.ppermute(x, AXES, pairs)]
    ppermute x0 -> x33, starting transfers between devices: none -> 49.9 us  [move(): return lax.ppermute(x, AXES, pairs)]
    reduce_sum x14 -> x0, other arithmetic: 46.3 us -> none  [the longest x8 41.6 us: per_block(): total_new = total_old * factor + jnp.sum(weights, axis=-1)]
    psum x1 -> x0, waiting for transfers between devices: 34.9 us -> none  [from_root(): return lax.psum(block, axis)]
    all_to_all x6, blocking collectives: 116 us -> 84.4 us  [exchange(): lax.all_to_all(x, AXES, 0, 0, tiled=True, axis_index_groups=group_lists())]
  transfers between devices with their start and end apart: 11 -> 33, of which waited for: 10 -> 20; matrix products, arithmetic and copies ran while one was open for 2% -> 0% of each run, Pallas kernels for 0% -> 0%
where the time goes in v1:
time: 261 us
  blocking collectives  84.4 us (32%)
  Pallas kernels  59.6 us (23%)
  waiting for transfers between devices  56.1 us (21%)
  starting transfers between devices  49.9 us (19%)
  local copies, waits for them, and re-layouts  9.52 us (4%)
    all_to_all x6, blocking collectives, exchange(): lax.all_to_all(x, AXES, 0, 0, tiled=True, axis_index_groups=group_lists())  84.4 us
    ppermute x33, waiting for transfers between devices, move(): return lax.ppermute(x, AXES, pairs)  56.1 us
    ppermute x33, starting transfers between devices, move(): return lax.ppermute(x, AXES, pairs)  49.9 us
    pallas_call x2, Pallas kernels, attend(): pl.pallas_call(body, in_specs=[SM] + [VM] * (1 + len(blocks)), out_specs=...  39.9 us
    unnamed x44, local copies, waits for them, and re-layouts  9.27 us
    pallas_call x1, Pallas kernels, second_projection(): pl.pallas_call(second_body, grid=(heads // 2,), in_specs=[SM, SM, SM] + [...  7.24 us
    pallas_call x2, Pallas kernels, out_projection(): pl.pallas_call(body, grid=(COLS // width,), in_specs=[SM, SM, SM] + [whol...  6.06 us
  transfers between devices with their start and end apart: 33, of which 20 were waited for; matrix products, arithmetic and copies ran while one was open for 0% of the time, Pallas kernels for 0%

profile of v1, /device:TPU:1, one launch (start us, length us, event | category | flops | bytes accessed | tf_op | source)
XLA Modules:
  0.0 260.6 jit_solution(7550572734376197829)
XLA Ops:
  0.6 3.7 %collective-permute-start.1 = (bf16[64,3072]{1,0:T(8,128)(2,1)}, bf16[64,3072]{1,0:T(8,128)(2,1)S(1)}, u32[]{:S(2)}, u32[]{:S(2)}) collective-permute-start(bf16[64,3072]{1,0:T(8,128)(2,1)} %bitcast.25), channel_id=1, source_target_pairs={{0,64},{1,65},{2,66},{3,67},{4,68},{5,69},{6,70},{7,71},{8,72},{9,... | collective-permute-start | bytes 1179656 | tf_op jit(solution)/shard_map/ppermute | solution.py:45
  5.2 7.6 %collective-permute-done.1.x2 = bf16[64,3072]{1,0:T(8,128)(2,1)S(1)} collective-permute-done((bf16[64,3072]{1,0:T(8,128)(2,1)}, bf16[64,3072]{1,0:T(8,128)(2,1)S(1)}, u32[]{:S(2)}, u32[]{:S(2)}) %collective-permute-start.1) | collective-permute-done | bytes 393248 | tf_op jit(solution)/shard_map/ppermute | solution.py:45
  15.9 3.2 %copy-done = bf16[3072,1280]{1,0:T(8,128)(2,1)S(1)} copy-done((bf16[3072,1280]{1,0:T(8,128)(2,1)S(1)}, bf16[3072,1280]{1,0:T(8,128)(2,1)}, u32[]{:S(2)}) %copy-start) | copy-done | bytes 7864344
  22.5 5.2 %modulate_project.1 = (bf16[10,128,128]{2,1,0:T(8,128)(2,1)S(1)}, bf16[10,128,128]{2,1,0:T(8,128)(2,1)S(1)}) custom-call(s32[1]{0:T(128)} %bitcast.pos.refs_0_, s32[4]{0:T(128)S(1)} %copy-done.7, s32[4]{0:T(128)S(1)} %copy-done.9, bf16[64,3072]{1,0:T(8,128)(2,1)S(1)} %bitcast.27, bf16[64,3072]{1,0:T(8,128)(2,1)S(1)} %collective-permute-done.x1, ...), custom_call_target="tpu_custom_call" | custom-call | tf_op jit(solution)/shard_map/modulate_project/pallas_call | solution.py:179
  29.5 13.7 %all_to_all.30 = bf16[8,2,128,128]{3,2,1,0:T(8,128)(2,1)S(1)} all-to-all(bf16[8,2,128,128]{3,2,1,0:T(8,128)(2,1)S(1)} %get-tuple-element.15), channel_id=1, replica_groups={{0,1,4,5,64,65,68,69},{2,3,6,7,66,67,70,71},{8,9,12,13,72,73,76,77},{10..., dimensions={0} | all-to-all | bytes 1048576 | tf_op jit(solution)/shard_map/all_to_all | solution.py:65
  52.0 3.4 %collective-permute-done.7 = bf16[2,2,128,128]{3,2,1,0:T(8,128)(2,1)S(1)} collective-permute-done((bf16[2,2,128,128]{3,2,1,0:T(8,128)(2,1)S(1)}, bf16[2,2,128,128]{3,2,1,0:T(8,128)(2,1)S(1)}, u32[]{:S(2)}, u32[]{:S(2)}) %collective-permute-start.7) | collective-permute-done | bytes 131104 | tf_op jit(solution)/shard_map/ppermute | solution.py:45
  58.1 3.2 %collective-permute-done.9 = bf16[4,2,128,128]{3,2,1,0:T(8,128)(2,1)S(1)} collective-permute-done((bf16[4,2,128,128]{3,2,1,0:T(8,128)(2,1)S(1)}, bf16[4,2,128,128]{3,2,1,0:T(8,128)(2,1)S(1)}, u32[]{:S(2)}, u32[]{:S(2)}) %collective-permute-start.9) | collective-permute-done | bytes 262176 | tf_op jit(solution)/shard_map/ppermute | solution.py:45
  61.3 3.6 %collective-permute-done.10 = bf16[4,2,128,128]{3,2,1,0:T(8,128)(2,1)S(1)} collective-permute-done((bf16[4,2,128,128]{3,2,1,0:T(8,128)(2,1)S(1)}, bf16[4,2,128,128]{3,2,1,0:T(8,128)(2,1)S(1)}, u32[]{:S(2)}, u32[]{:S(2)}) %collective-permute-start.10) | collective-permute-done | bytes 262176 | tf_op jit(solution)/shard_map/ppermute | solution.py:45
  67.0 5.0 %collective-permute-start.13 = (bf16[20,2,128,128]{3,2,1,0:T(8,128)(2,1)S(1)}, bf16[20,2,128,128]{3,2,1,0:T(8,128)(2,1)S(1)}, u32[]{:S(2)}, u32[]{:S(2)}) collective-permute-start(bf16[20,2,128,128]{3,2,1,0:T(8,128)(2,1)S(1)} %constant_dynamic-update-slice_fusion.4.refs_4_), channel_id=1, source_target_pairs={{0,32},{1,33},{2,34},{3,35},{4,36},{5,37},{6,38},{7,39},{8,40},{9,... | collective-permute-start | bytes 3932168 | tf_op jit(solution)/shard_map/ppermute | solution.py:45
  72.2 15.1 %all_to_all.31.refs_1_ = bf16[8,3,128,128]{3,2,1,0:T(8,128)(2,1)S(1)} all-to-all(bf16[8,3,128,128]{3,2,1,0:T(8,128)(2,1)S(1)} %bitcast.29), channel_id=1, replica_groups={{0,1,4,5,64,65,68,69},{2,3,6,7,66,67,70,71},{8,9,12,13,72,73,76,77},{10..., dimensions={0} | all-to-all | bytes 1572864 | tf_op jit(solution)/shard_map/all_to_all | solution.py:65
  87.3 19.9 %span_attention.2 = bf16[8,3,128,128]{3,2,1,0:T(8,128)(2,1)S(1)} custom-call(s32[4]{0:T(128)S(1)} %copy-done.8, bf16[8,3,128,128]{3,2,1,0:T(8,128)(2,1)S(1)} %all_to_all.31.refs_1_, bf16[12,2,128,128]{3,2,1,0:T(8,128)(2,1)S(1)} %constant_dynamic-update-slice_fusion.refs_2_, bf16[12,2,128,128]{3,2,1,0:T(8,128)(2,1)S(1)} %collective-permute-done.8.refs_3_, ...), custom_call_target="tpu_custom_call" | custom-call | tf_op jit(solution)/shard_map/span_attention/pallas_call | solution.py:318
  107.3 14.6 %all_to_all.32 = bf16[8,3,128,128]{3,2,1,0:T(8,128)(2,1)S(1)} all-to-all(bf16[8,3,128,128]{3,2,1,0:T(8,128)(2,1)S(1)} %span_attention.2), channel_id=1, replica_groups={{0,1,4,5,64,65,68,69},{2,3,6,7,66,67,70,71},{8,9,12,13,72,73,76,77},{10..., dimensions={0} | all-to-all | bytes 1572864 | tf_op jit(solution)/shard_map/all_to_all | solution.py:65
  128.8 3.0 %out_projection.2.v0 = bf16[256,768]{1,0:T(8,128)(2,1)S(1)} custom-call(s32[1]{0:T(128)} %bitcast.pos.refs_0_, s32[4]{0:T(128)S(1)} %copy-done.8, s32[4]{0:T(128)S(1)} %copy-done.10, bf16[24,128,128]{2,1,0:T(8,128)(2,1)S(1)} %bitcast.22, bf16[24,128,128]{2,1,0:T(8,128)(2,1)S(1)} %collective-permute-done.14.refs_4_, f32[9,3,3072]{2,1,0:T(4,128)S(1)} %copy-done.3, ...), custom_call_target="tpu_custom_call" | custom-call | tf_op jit(solution)/shard_map/out_projection/pallas_call | solution.py:373
  133.7 10.0 %collective-permute-done.16.v2 = bf16[256,768]{1,0:T(8,128)(2,1)S(1)} collective-permute-done((bf16[256,768]{1,0:T(8,128)(2,1)S(1)}, bf16[256,768]{1,0:T(8,128)(2,1)S(1)}, u32[]{:S(2)}, u32[]{:S(2)}) %collective-permute-start.16) | collective-permute-done | bytes 393248 | tf_op jit(solution)/shard_map/ppermute | solution.py:45
  146.3 7.2 %advance_modulate_project.1 = (bf16[10,128,128]{2,1,0:T(8,128)(2,1)S(1)}, bf16[10,128,128]{2,1,0:T(8,128)(2,1)S(1)}, bf16[64,3072]{1,0:T(8,128)(2,1)S(1)}, bf16[64,768]{1,0:T(8,128)(2,1)}) custom-call(s32[1]{0:T(128)} %bitcast.pos.refs_0_, s32[4]{0:T(128)S(1)} %copy-done.8, s32[4]{0:T(128)S(1)} %copy-done.10, bf16[64,3072]{1,0:T(8,128)(2,1)S(1)} %bitcast.28, ...), custom_call_target="tpu_custom_call" | custom-call | tf_op jit(solution)/shard_map/advance_modulate_project/pallas_call | solution.py:195
  155.4 11.2 %all_to_all.33 = bf16[8,2,128,128]{3,2,1,0:T(8,128)(2,1)S(1)} all-to-all(bf16[8,2,128,128]{3,2,1,0:T(8,128)(2,1)S(1)} %get-tuple-element.20), channel_id=1, replica_groups={{0,1,4,5,64,65,68,69},{2,3,6,7,66,67,70,71},{8,9,12,13,72,73,76,77},{10..., dimensions={0} | all-to-all | bytes 1048576 | tf_op jit(solution)/shard_map/all_to_all | solution.py:65
  173.9 3.1 %collective-permute-done.22 = bf16[2,2,128,128]{3,2,1,0:T(8,128)(2,1)S(1)} collective-permute-done((bf16[2,2,128,128]{3,2,1,0:T(8,128)(2,1)S(1)}, bf16[2,2,128,128]{3,2,1,0:T(8,128)(2,1)S(1)}, u32[]{:S(2)}, u32[]{:S(2)}) %collective-permute-start.22) | collective-permute-done | bytes 131104 | tf_op jit(solution)/shard_map/ppermute | solution.py:45
  179.5 3.6 %collective-permute-done.24 = bf16[4,2,128,128]{3,2,1,0:T(8,128)(2,1)S(1)} collective-permute-done((bf16[4,2,128,128]{3,2,1,0:T(8,128)(2,1)S(1)}, bf16[4,2,128,128]{3,2,1,0:T(8,128)(2,1)S(1)}, u32[]{:S(2)}, u32[]{:S(2)}) %collective-permute-start.24) | collective-permute-done | bytes 262176 | tf_op jit(solution)/shard_map/ppermute | solution.py:45
  184.6 3.6 %collective-permute-done.26 = bf16[4,2,128,128]{3,2,1,0:T(8,128)(2,1)S(1)} collective-permute-done((bf16[4,2,128,128]{3,2,1,0:T(8,128)(2,1)S(1)}, bf16[4,2,128,128]{3,2,1,0:T(8,128)(2,1)S(1)}, u32[]{:S(2)}, u32[]{:S(2)}) %collective-permute-start.26) | collective-permute-done | bytes 262176 | tf_op jit(solution)/shard_map/ppermute | solution.py:45
  188.3 5.2 %collective-permute-start.28 = (bf16[20,2,128,128]{3,2,1,0:T(8,128)(2,1)S(1)}, bf16[20,2,128,128]{3,2,1,0:T(8,128)(2,1)S(1)}, u32[]{:S(2)}, u32[]{:S(2)}) collective-permute-start(bf16[20,2,128,128]{3,2,1,0:T(8,128)(2,1)S(1)} %constant_dynamic-update-slice_fusion.12.refs_4_), channel_id=1, source_target_pairs={{0,32},{1,33},{2,34},{3,35},{4,36},{5,37},{6,38},{7,39},{8,40},{9,... | collective-permute-start | bytes 3932168 | tf_op jit(solution)/shard_map/ppermute | solution.py:45
  193.7 15.3 %all_to_all.34.refs_1_ = bf16[8,3,128,128]{3,2,1,0:T(8,128)(2,1)S(1)} all-to-all(bf16[8,3,128,128]{3,2,1,0:T(8,128)(2,1)S(1)} %bitcast.30), channel_id=1, replica_groups={{0,1,4,5,64,65,68,69},{2,3,6,7,66,67,70,71},{8,9,12,13,72,73,76,77},{10..., dimensions={0} | all-to-all | bytes 1572864 | tf_op jit(solution)/shard_map/all_to_all | solution.py:65
  209.0 20.0 %span_attention.3 = bf16[8,3,128,128]{3,2,1,0:T(8,128)(2,1)S(1)} custom-call(s32[4]{0:T(128)S(1)} %copy-done.8, bf16[8,3,128,128]{3,2,1,0:T(8,128)(2,1)S(1)} %all_to_all.34.refs_1_, bf16[12,2,128,128]{3,2,1,0:T(8,128)(2,1)S(1)} %constant_dynamic-update-slice_fusion.8.refs_2_, bf16[12,2,128,128]{3,2,1,0:T(8,128)(2,1)S(1)} %collective-permute-done.23.refs_3_, ...), custom_call_target="tpu_custom_call" | custom-call | tf_op jit(solution)/shard_map/span_attention/pallas_call | solution.py:318
  229.0 14.4 %all_to_all.35 = bf16[8,3,128,128]{3,2,1,0:T(8,128)(2,1)S(1)} all-to-all(bf16[8,3,128,128]{3,2,1,0:T(8,128)(2,1)S(1)} %span_attention.3), channel_id=1, replica_groups={{0,1,4,5,64,65,68,69},{2,3,6,7,66,67,70,71},{8,9,12,13,72,73,76,77},{10..., dimensions={0} | all-to-all | bytes 1572864 | tf_op jit(solution)/shard_map/all_to_all | solution.py:65
  248.0 3.0 %out_projection.3 = bf16[4,64,768]{2,1,0:T(8,128)(2,1)S(1)} custom-call(s32[1]{0:T(128)} %bitcast.pos.refs_0_, s32[4]{0:T(128)S(1)} %copy-done.8, s32[4]{0:T(128)S(1)} %copy-done.10, bf16[24,128,128]{2,1,0:T(8,128)(2,1)S(1)} %bitcast.24, bf16[24,128,128]{2,1,0:T(8,128)(2,1)S(1)} %collective-permute-done.29.refs_4_, f32[9,3,3072]{2,1,0:T(4,128)S(1)} %copy-done.3, ...), custom_call_target="tpu_custom_call" | custom-call | tf_op jit(solution)/shard_map/out_projection/pallas_call | solution.py:373
  (114 shorter events, 61.7 us)
Async XLA Ops:
  0.6 12.2 %collective-permute-start.1 = (bf16[64,3072]{1,0:T(8,128)(2,1)}, bf16[64,3072]{1,0:T(8,128)(2,1)S(1)}, u32[]{:S(2)}, u32[]{:S(2)}) collective-permute-start(bf16[64,3072]{1,0:T(8,128)(2,1)} %bitcast.25), channel_id=1, source_target_pairs={{0,64},{1,65},{2,66},{3,67},{4,68},{5,69},{6,70},{7,71},{8,72},{9,... | collective-permute-start | bytes 1179656 | tf_op jit(solution)/shard_map/ppermute | solution.py:45
  4.3 10.3 %collective-permute-start = (bf16[64,3072]{1,0:T(8,128)(2,1)}, bf16[64,3072]{1,0:T(8,128)(2,1)S(1)}, u32[]{:S(2)}, u32[]{:S(2)}) collective-permute-start(bf16[64,3072]{1,0:T(8,128)(2,1)} %bitcast.26), channel_id=1, source_target_pairs={{0,32},{1,33},{2,34},{3,35},{4,36},{5,37},{6,38},{7,39},{8,40},{9,... | collective-permute-start | bytes 1179656 | tf_op jit(solution)/shard_map/ppermute | solution.py:45
  43.2 7.8 %collective-permute-start.4 = (bf16[2,2,128,128]{3,2,1,0:T(8,128)(2,1)S(1)}, bf16[2,2,128,128]{3,2,1,0:T(8,128)(2,1)S(1)}, u32[]{:S(2)}, u32[]{:S(2)}) collective-permute-start(bf16[2,2,128,128]{3,2,1,0:T(8,128)(2,1)S(1)} %get-tuple-element.27), channel_id=1, source_target_pairs={{0,2},{1,3},{2,0},{3,1},{4,6},{5,7},{6,4},{7,5},{8,10},{9,11},{10,... | collective-permute-start | bytes 393224 | tf_op jit(solution)/shard_map/ppermute | solution.py:45
  45.9 6.1 %collective-permute-start.5 = (bf16[2,2,128,128]{3,2,1,0:T(8,128)(2,1)S(1)}, bf16[2,2,128,128]{3,2,1,0:T(8,128)(2,1)S(1)}, u32[]{:S(2)}, u32[]{:S(2)}) collective-permute-start(bf16[2,2,128,128]{3,2,1,0:T(8,128)(2,1)S(1)} %get-tuple-element.26), channel_id=1, source_target_pairs={{0,8},{1,9},{2,10},{3,11},{4,12},{5,13},{6,14},{7,15},{8,16},{9,17... | collective-permute-start | bytes 393224 | tf_op jit(solution)/shard_map/ppermute | solution.py:45
  49.7 5.8 %collective-permute-start.7 = (bf16[2,2,128,128]{3,2,1,0:T(8,128)(2,1)S(1)}, bf16[2,2,128,128]{3,2,1,0:T(8,128)(2,1)S(1)}, u32[]{:S(2)}, u32[]{:S(2)}) collective-permute-start(bf16[2,2,128,128]{3,2,1,0:T(8,128)(2,1)S(1)} %get-tuple-element.26), channel_id=1, source_target_pairs={{0,16},{1,17},{2,18},{3,19},{4,20},{5,21},{6,22},{7,23},{8,24},{9,... | collective-permute-start | bytes 393224 | tf_op jit(solution)/shard_map/ppermute | solution.py:45
  51.0 10.3 %collective-permute-start.9 = (bf16[4,2,128,128]{3,2,1,0:T(8,128)(2,1)S(1)}, bf16[4,2,128,128]{3,2,1,0:T(8,128)(2,1)S(1)}, u32[]{:S(2)}, u32[]{:S(2)}) collective-permute-start(bf16[4,2,128,128]{3,2,1,0:T(8,128)(2,1)S(1)} %pad_maximum_fusion.2), channel_id=1, source_target_pairs={{0,8},{1,9},{2,10},{3,11},{4,12},{5,13},{6,14},{7,15},{8,16},{9,17... | collective-permute-start | bytes 786440 | tf_op jit(solution)/shard_map/ppermute | solution.py:45
  55.6 11.3 %collective-permute-start.12 = (bf16[8,2,128,128]{3,2,1,0:T(8,128)(2,1)S(1)}, bf16[8,2,128,128]{3,2,1,0:T(8,128)(2,1)S(1)}, u32[]{:S(2)}, u32[]{:S(2)}) collective-permute-start(bf16[8,2,128,128]{3,2,1,0:T(8,128)(2,1)S(1)} %pad_maximum_fusion), channel_id=1, source_target_pairs={{0,2},{1,3},{2,0},{3,1},{4,6},{5,7},{6,4},{7,5},{8,10},{9,11},{10,... | collective-permute-start | bytes 1572872 | tf_op jit(solution)/shard_map/ppermute | solution.py:45
  56.0 9.0 %collective-permute-start.10 = (bf16[4,2,128,128]{3,2,1,0:T(8,128)(2,1)S(1)}, bf16[4,2,128,128]{3,2,1,0:T(8,128)(2,1)S(1)}, u32[]{:S(2)}, u32[]{:S(2)}) collective-permute-start(bf16[4,2,128,128]{3,2,1,0:T(8,128)(2,1)S(1)} %pad_maximum_fusion.2), channel_id=1, source_target_pairs={{0,24},{1,25},{2,26},{3,27},{4,28},{5,29},{6,30},{7,31},{8,0},{9,1... | collective-permute-start | bytes 786440 | tf_op jit(solution)/shard_map/ppermute | solution.py:45
  58.1 8.8 %collective-permute-start.11 = (bf16[4,2,128,128]{3,2,1,0:T(8,128)(2,1)S(1)}, bf16[4,2,128,128]{3,2,1,0:T(8,128)(2,1)S(1)}, u32[]{:S(2)}, u32[]{:S(2)}) collective-permute-start(bf16[4,2,128,128]{3,2,1,0:T(8,128)(2,1)S(1)} %pad_maximum_fusion.2), channel_id=1, source_target_pairs={{0,16},{1,17},{2,18},{3,19},{4,20},{5,21},{6,22},{7,23},{8,24},{9,... | collective-permute-start | bytes 786440 | tf_op jit(solution)/shard_map/ppermute | solution.py:45
  67.0 20.3 %collective-permute-start.13 = (bf16[20,2,128,128]{3,2,1,0:T(8,128)(2,1)S(1)}, bf16[20,2,128,128]{3,2,1,0:T(8,128)(2,1)S(1)}, u32[]{:S(2)}, u32[]{:S(2)}) collective-permute-start(bf16[20,2,128,128]{3,2,1,0:T(8,128)(2,1)S(1)} %constant_dynamic-update-slice_fusion.4.refs_4_), channel_id=1, source_target_pairs={{0,32},{1,33},{2,34},{3,35},{4,36},{5,37},{6,38},{7,39},{8,40},{9,... | collective-permute-start | bytes 3932168 | tf_op jit(solution)/shard_map/ppermute | solution.py:45
  72.1 15.2 %collective-permute-start.8 = (bf16[12,2,128,128]{3,2,1,0:T(8,128)(2,1)S(1)}, bf16[12,2,128,128]{3,2,1,0:T(8,128)(2,1)S(1)}, u32[]{:S(2)}, u32[]{:S(2)}) collective-permute-start(bf16[12,2,128,128]{3,2,1,0:T(8,128)(2,1)S(1)} %constant_dynamic-update-slice_fusion.refs_2_), channel_id=1, source_target_pairs={{0,32},{1,33},{2,34},{3,35},{4,36},{5,37},{6,38},{7,39},{8,40},{9,... | collective-permute-start | bytes 2359304 | tf_op jit(solution)/shard_map/ppermute | solution.py:45
  131.8 11.9 %collective-permute-start.16 = (bf16[256,768]{1,0:T(8,128)(2,1)S(1)}, bf16[256,768]{1,0:T(8,128)(2,1)S(1)}, u32[]{:S(2)}, u32[]{:S(2)}) collective-permute-start(bf16[256,768]{1,0:T(8,128)(2,1)S(1)} %out_projection.2.v0), channel_id=1, source_target_pairs={{0,64},{1,65},{2,66},{3,67},{4,68},{5,69},{6,70},{7,71},{8,72},{9,... | collective-permute-start | bytes 1179656 | tf_op jit(solution)/shard_map/ppermute | solution.py:45
  133.1 11.9 %collective-permute-start.15 = (bf16[256,768]{1,0:T(8,128)(2,1)S(1)}, bf16[256,768]{1,0:T(8,128)(2,1)S(1)}, u32[]{:S(2)}, u32[]{:S(2)}) collective-permute-start(bf16[256,768]{1,0:T(8,128)(2,1)S(1)} %out_projection.2.v0), channel_id=1, source_target_pairs={{0,32},{1,33},{2,34},{3,35},{4,36},{5,37},{6,38},{7,39},{8,40},{9,... | collective-permute-start | bytes 1179656 | tf_op jit(solution)/shard_map/ppermute | solution.py:45
  166.6 5.8 %collective-permute-start.19 = (bf16[2,2,128,128]{3,2,1,0:T(8,128)(2,1)S(1)}, bf16[2,2,128,128]{3,2,1,0:T(8,128)(2,1)S(1)}, u32[]{:S(2)}, u32[]{:S(2)}) collective-permute-start(bf16[2,2,128,128]{3,2,1,0:T(8,128)(2,1)S(1)} %get-tuple-element.25), channel_id=1, source_target_pairs={{0,2},{1,3},{2,0},{3,1},{4,6},{5,7},{6,4},{7,5},{8,10},{9,11},{10,... | collective-permute-start | bytes 393224 | tf_op jit(solution)/shard_map/ppermute | solution.py:45
  168.3 5.6 %collective-permute-start.20 = (bf16[2,2,128,128]{3,2,1,0:T(8,128)(2,1)S(1)}, bf16[2,2,128,128]{3,2,1,0:T(8,128)(2,1)S(1)}, u32[]{:S(2)}, u32[]{:S(2)}) collective-permute-start(bf16[2,2,128,128]{3,2,1,0:T(8,128)(2,1)S(1)} %get-tuple-element.24), channel_id=1, source_target_pairs={{0,8},{1,9},{2,10},{3,11},{4,12},{5,13},{6,14},{7,15},{8,16},{9,17... | collective-permute-start | bytes 393224 | tf_op jit(solution)/shard_map/ppermute | solution.py:45
  171.2 5.8 %collective-permute-start.22 = (bf16[2,2,128,128]{3,2,1,0:T(8,128)(2,1)S(1)}, bf16[2,2,128,128]{3,2,1,0:T(8,128)(2,1)S(1)}, u32[]{:S(2)}, u32[]{:S(2)}) collective-permute-start(bf16[2,2,128,128]{3,2,1,0:T(8,128)(2,1)S(1)} %get-tuple-element.24), channel_id=1, source_target_pairs={{0,16},{1,17},{2,18},{3,19},{4,20},{5,21},{6,22},{7,23},{8,24},{9,... | collective-permute-start | bytes 393224 | tf_op jit(solution)/shard_map/ppermute | solution.py:45
  172.5 10.6 %collective-permute-start.24 = (bf16[4,2,128,128]{3,2,1,0:T(8,128)(2,1)S(1)}, bf16[4,2,128,128]{3,2,1,0:T(8,128)(2,1)S(1)}, u32[]{:S(2)}, u32[]{:S(2)}) collective-permute-start(bf16[4,2,128,128]{3,2,1,0:T(8,128)(2,1)S(1)} %pad_maximum_fusion.3), channel_id=1, source_target_pairs={{0,8},{1,9},{2,10},{3,11},{4,12},{5,13},{6,14},{7,15},{8,16},{9,17... | collective-permute-start | bytes 786440 | tf_op jit(solution)/shard_map/ppermute | solution.py:45
  177.1 11.1 %collective-permute-start.27 = (bf16[8,2,128,128]{3,2,1,0:T(8,128)(2,1)S(1)}, bf16[8,2,128,128]{3,2,1,0:T(8,128)(2,1)S(1)}, u32[]{:S(2)}, u32[]{:S(2)}) collective-permute-start(bf16[8,2,128,128]{3,2,1,0:T(8,128)(2,1)S(1)} %pad_maximum_fusion.1), channel_id=1, source_target_pairs={{0,2},{1,3},{2,0},{3,1},{4,6},{5,7},{6,4},{7,5},{8,10},{9,11},{10,... | collective-permute-start | bytes 1572872 | tf_op jit(solution)/shard_map/ppermute | solution.py:45
  179.0 5.5 %collective-permute-start.25 = (bf16[4,2,128,128]{3,2,1,0:T(8,128)(2,1)S(1)}, bf16[4,2,128,128]{3,2,1,0:T(8,128)(2,1)S(1)}, u32[]{:S(2)}, u32[]{:S(2)}) collective-permute-start(bf16[4,2,128,128]{3,2,1,0:T(8,128)(2,1)S(1)} %pad_maximum_fusion.3), channel_id=1, source_target_pairs={{0,24},{1,25},{2,26},{3,27},{4,28},{5,29},{6,30},{7,31},{8,0},{9,1... | collective-permute-start | bytes 786440 | tf_op jit(solution)/shard_map/ppermute | solution.py:45
  179.4 8.8 %collective-permute-start.26 = (bf16[4,2,128,128]{3,2,1,0:T(8,128)(2,1)S(1)}, bf16[4,2,128,128]{3,2,1,0:T(8,128)(2,1)S(1)}, u32[]{:S(2)}, u32[]{:S(2)}) collective-permute-start(bf16[4,2,128,128]{3,2,1,0:T(8,128)(2,1)S(1)} %pad_maximum_fusion.3), channel_id=1, source_target_pairs={{0,16},{1,17},{2,18},{3,19},{4,20},{5,21},{6,22},{7,23},{8,24},{9,... | collective-permute-start | bytes 786440 | tf_op jit(solution)/shard_map/ppermute | solution.py:45
  188.3 20.7 %collective-permute-start.28 = (bf16[20,2,128,128]{3,2,1,0:T(8,128)(2,1)S(1)}, bf16[20,2,128,128]{3,2,1,0:T(8,128)(2,1)S(1)}, u32[]{:S(2)}, u32[]{:S(2)}) collective-permute-start(bf16[20,2,128,128]{3,2,1,0:T(8,128)(2,1)S(1)} %constant_dynamic-update-slice_fusion.12.refs_4_), channel_id=1, source_target_pairs={{0,32},{1,33},{2,34},{3,35},{4,36},{5,37},{6,38},{7,39},{8,40},{9,... | collective-permute-start | bytes 3932168 | tf_op jit(solution)/shard_map/ppermute | solution.py:45
  193.6 15.4 %collective-permute-start.23 = (bf16[12,2,128,128]{3,2,1,0:T(8,128)(2,1)S(1)}, bf16[12,2,128,128]{3,2,1,0:T(8,128)(2,1)S(1)}, u32[]{:S(2)}, u32[]{:S(2)}) collective-permute-start(bf16[12,2,128,128]{3,2,1,0:T(8,128)(2,1)S(1)} %constant_dynamic-update-slice_fusion.8.refs_2_), channel_id=1, source_target_pairs={{0,32},{1,33},{2,34},{3,35},{4,36},{5,37},{6,38},{7,39},{8,40},{9,... | collective-permute-start | bytes 2359304 | tf_op jit(solution)/shard_map/ppermute | solution.py:45
  251.5 5.8 %collective-permute-start.31 = (bf16[64,768]{1,0:T(8,128)(2,1)S(1)}, bf16[64,768]{1,0:T(8,128)(2,1)S(1)}, u32[]{:S(2)}, u32[]{:S(2)}) collective-permute-start(bf16[64,768]{1,0:T(8,128)(2,1)S(1)} %get-tuple-element.29), channel_id=1, source_target_pairs={{0,64},{1,65},{2,66},{3,67},{4,68},{5,69},{6,70},{7,71},{8,72},{9,... | collective-permute-start | bytes 294920 | tf_op jit(solution)/shard_map/ppermute | solution.py:45
  252.7 6.9 %collective-permute-start.32 = (bf16[64,768]{1,0:T(8,128)(2,1)S(1)}, bf16[64,768]{1,0:T(8,128)(2,1)S(1)}, u32[]{:S(2)}, u32[]{:S(2)}) collective-permute-start(bf16[64,768]{1,0:T(8,128)(2,1)S(1)} %get-tuple-element.28), channel_id=1, source_target_pairs={{0,96},{1,97},{2,98},{3,99},{4,100},{5,101},{6,102},{7,103},{8,104... | collective-permute-start | bytes 294920 | tf_op jit(solution)/shard_map/ppermute | solution.py:45
  (24 other events, 402.3 us)

commit v2 on v1

v2 whole, which is shorter than its diff:
```python
import math

import jax
import jax.numpy as jnp
from jax import lax
from jax.experimental import pallas as pl
from jax.experimental.pallas import tpu as pltpu
from jax.sharding import PartitionSpec as P

HD = 128
EPS = 1e-06
BF = jnp.bfloat16
F32 = jnp.float32
AXES = ("slot", "ctx")
VM = pl.BlockSpec(memory_space=pltpu.VMEM)
SM = pl.BlockSpec(memory_space=pltpu.SMEM)
SLOTS = 4
PER = 2
TOK = 64
HALF = 32
ROWS = SLOTS * HALF
WIDTH = 3072
COLS = WIDTH // SLOTS
LOG2E = 1.4426950408889634


def where_is(flat):
    s, c = flat // 32, flat % 32
    return dict(h=s // 2, i=s % 2, z=c // 8, xl=(c // 4) % 2, y=c % 4)


def flat_of(d):
    return (d["h"] * 2 + d["i"]) * 32 + d["z"] * 8 + d["xl"] * 4 + d["y"]


def move(x, h=0, i=0, z=0, y=0):
    pairs = []
    for f in range(128):
        d = where_is(f)
        d["h"] = (d["h"] + h) % 2
        d["i"] = (d["i"] + i) % 2
        d["z"] = (d["z"] + z) % 4
        d["y"] = (d["y"] + y) % 4
        pairs.append((f, flat_of(d)))
    return lax.ppermute(x, AXES, pairs)


def group_lists():
    out = []
    for i in range(2):
        for z in range(4):
            for yh in range(2):
                out.append(
                    [
                        flat_of(dict(h=h, i=i, z=z, xl=xl, y=2 * yh + yl))
                        for h in range(2)
                        for xl in range(2)
                        for yl in range(2)
                    ]
                )
    return out


def exchange(x):
    return lax.all_to_all(x, AXES, 0, 0, tiled=True, axis_index_groups=group_lists())


def params(mib, **kw):
    return pltpu.CompilerParams(vmem_limit_bytes=mib * 1024 * 1024, **kw)


def first_slot(sc):
    best, at = sc[0], jnp.int32(0)
    for j in range(1, SLOTS):
        less = sc[j] < best
        best = jnp.where(less, sc[j], best)
        at = jnp.where(less, j, at)
    return at


def id_of(sc, t, step):
    if step == 0:
        return sc[t]
    return jnp.where(first_slot(sc) == t, SLOTS, sc[t])


def level_of(sc, t, step):
    mine = sc[t]
    rank = jnp.int32(0)
    for j in range(SLOTS):
        rank = rank + (sc[j] < mine).astype(jnp.int32)
    level = PER * rank + sc[SLOTS + t] + 1
    if step == 0:
        return level
    return jnp.where(rank == 0, SLOTS * PER, level - 1)


def row_of(half, slot):
    return pl.ds(pl.multiple_of((half * SLOTS + slot) * HALF, HALF), HALF)


def col_of(slot, width=COLS):
    return pl.ds(pl.multiple_of(slot * width, 128), width)


def modulated(values, ada, level):
    center = jnp.mean(values, axis=-1, keepdims=True)
    off = values - center
    spread = jnp.mean(off * off, axis=-1, keepdims=True)
    normed = off * lax.rsqrt(spread + EPS)
    return (normed * (1.0 + ada[level, 1:2, :]) + ada[level, 0:1, :]).astype(BF)


def project(hidden, w, mine, theirs):
    out = jnp.dot(hidden[...], w[...], preferred_element_type=F32).astype(BF)
    cut = out.shape[0] // 2
    for k in range(2):
        mine[k] = out[:cut, k * HD : (k + 1) * HD]
        theirs[k] = out[cut:, k * HD : (k + 1) * HD]


def first_body(sc, x0, x1, ada, w, mine, theirs, hidden, *, far):
    s = sc[8]
    i = s % 2

    @pl.when(pl.program_id(0) == 0)
    def _():
        for r, x in enumerate((x0, x1)):
            t = s ^ (r + far)
            level = level_of(sc, t, 0)
            for a in range(2):
                values = x[a * HALF : (a + 1) * HALF, :].astype(F32)
                at = pl.multiple_of(((i ^ a) * 2 + t % 2) * HALF, HALF)
                hidden[pl.ds(at, HALF), :] = modulated(values, ada, level)

    project(hidden, w, mine, theirs)


def second_body(
    sc, x0, x1, x2, x3, v0, v1, v2, v3, fresh, ada, w,
    mine, theirs, vel, fin, hidden, vall, moved,
):
    s = sc[8]
    i = s % 2

    @pl.when(pl.program_id(0) == 0)
    def _():
        for k, v in enumerate((v0, v1, v2, v3)):
            if k % 2 == 0:
                vall[:, col_of(s ^ k)] = v[...]
            else:
                vall[:ROWS, col_of(s ^ k)] = v[ROWS:, :]
                vall[ROWS:, col_of(s ^ k)] = v[:ROWS, :]
        first = first_slot(sc)
        for a in range(2):
            vel[a * HALF : (a + 1) * HALF, :] = vall[row_of(i ^ a, s), :]
        for r, x in enumerate((x0, x1, x2, x3)):
            t = s ^ r
            level = level_of(sc, t, 1)
            for a in range(2):
                rows = slice(a * HALF, (a + 1) * HALF)
                where = row_of(i ^ a, t)
                moved[...] = (
                    x[rows, :].astype(F32) - vall[where, :].astype(F32) * (1.0 / (SLOTS * PER))
                ).astype(BF)

                @pl.when(t == first)
                def _():
                    fin[rows, :] = moved[:, col_of(s)]
                    moved[...] = fresh[rows, :]

                hidden[where, :] = modulated(moved[...].astype(F32), ada, level)

    project(hidden, w, mine, theirs)


def whole(shape):
    return pl.BlockSpec(shape, lambda n: (0,) * len(shape))


def projected_shapes(heads, rows):
    return [jax.ShapeDtypeStruct((heads, rows, HD), BF)] * 2


def first_projection(sc, xs, far, ada, w):
    heads = w.shape[1] // HD

    def body(*refs):
        first_body(*refs, far=far)

    return pl.pallas_call(
        body,
        grid=(heads // 2,),
        in_specs=[SM]
        + [whole((TOK, WIDTH))] * 2
        + [whole(ada.shape), pl.BlockSpec((WIDTH, 2 * HD), lambda n: (0, n))],
        out_specs=[pl.BlockSpec((2, ROWS // 2, HD), lambda n: (n, 0, 0))] * 2,
        out_shape=projected_shapes(heads, ROWS // 2),
        scratch_shapes=[pltpu.VMEM((ROWS, WIDTH), BF)],
        compiler_params=params(24),
        cost_estimate=pl.CostEstimate(flops=4 * 10**9, bytes_accessed=10**7, transcendentals=0),
        name="modulate_project",
    )(sc, *xs, ada, w)


def second_projection(sc, xs, vs, fresh, ada, w):
    heads = w.shape[1] // HD
    return pl.pallas_call(
        second_body,
        grid=(heads // 2,),
        in_specs=[SM]
        + [whole((TOK, WIDTH))] * 4
        + [whole((2 * ROWS, COLS))] * 4
        + [whole((TOK, WIDTH)), whole(ada.shape), pl.BlockSpec((WIDTH, 2 * HD), lambda n: (0, n))],
        out_specs=[pl.BlockSpec((2, ROWS, HD), lambda n: (n, 0, 0))] * 2
        + [whole((TOK, WIDTH)), whole((TOK, COLS))],
        out_shape=projected_shapes(heads, ROWS)
        + [jax.ShapeDtypeStruct((TOK, WIDTH), BF), jax.ShapeDtypeStruct((TOK, COLS), BF)],
        scratch_shapes=[
            pltpu.VMEM((2 * ROWS, WIDTH), BF),
            pltpu.VMEM((2 * ROWS, WIDTH), BF),
            pltpu.VMEM((HALF, WIDTH), BF),
        ],
        compiler_params=params(40),
        name="advance_modulate_project",
    )(sc, *xs, *vs, fresh, ada, w)


def pack_body(sc, *refs):
    parts, (out, chip) = refs[:-2], refs[-2:]
    i, h = sc[8] % 2, sc[8] // 2
    for k in range(2):
        to = pl.ds(10 * jnp.where(k == 0, i, 1 - i), 10)
        if len(parts) == 2:
            chip[to] = parts[k][...]
        else:
            cut = ROWS // 2
            chip[to, pl.ds(pl.multiple_of(h * cut, cut), cut)] = parts[2 * k][...]
            chip[to, pl.ds(pl.multiple_of((1 - h) * cut, cut), cut)] = parts[2 * k + 1][...]
    for g in range(8):
        out[g, 3] = chip[4 + g]
        out[g, 4] = chip[12 + g]

    def queries(low, high, at):
        for n in range(24):
            if low <= n < high:
                out[n // 3, n % 3] = chip[n - at]
            else:
                out[n // 3, n % 3] = jnp.zeros((ROWS, HD), BF)

    @pl.when(h == 0)
    def _():
        queries(0, 20, 0)

    @pl.when(h != 0)
    def _():
        queries(20, 24, 20)


def pack(sc, *parts):
    return pl.pallas_call(
        pack_body,
        in_specs=[SM] + [VM] * len(parts),
        out_specs=VM,
        out_shape=jax.ShapeDtypeStruct((8, 5, ROWS, HD), BF),
        scratch_shapes=[pltpu.VMEM((20, ROWS, HD), BF)],
        compiler_params=params(16),
        name="pack_heads",
    )(sc, *parts)


QROWS = 4 * 3 * HALF
BLOCK = 128


def attend_body(step, parts, chunk, last, sc, q, *refs):
    blocks, refs = refs[:parts], refs[parts:]
    if last:
        top_in, acc_in, out, qs, ks, vs, tops, accs = refs
    else:
        tops, accs, qs, ks, vs = refs
    keys = ks.shape[1]
    at = 0
    for ref in blocks:
        for b in range(ref.shape[0]):
            for j in range(SLOTS):
                rows = slice(j * HALF, (j + 1) * HALF)
                ks[j, at * HALF : (at + 1) * HALF, :] = ref[b, 0, rows, :]
                vs[j, at * HALF : (at + 1) * HALF, :HD] = ref[b, 1, rows, :]
            at += 1
    vs[:, :, HD:] = jnp.ones((SLOTS, keys, HD), BF)
    factor = LOG2E / math.sqrt(HD)
    for c in range(4):
        for m in range(3):
            both = ((q[c, m].astype(F32) + q[4 + c, m].astype(F32)) * factor).astype(BF)
            for j in range(SLOTS):
                qs[j, (c * 3 + m) * HALF : (c * 3 + m + 1) * HALF, :] = both[j * HALF : (j + 1) * HALF]

    def per_span(t, _):
        if last:
            top, acc = tops, accs
            top[...] = top_in[t]
            acc[...] = acc_in[t]
        else:
            top, acc = tops.at[t], accs.at[t]
            top[...] = jnp.full(top.shape, -1e30, F32)
            acc[...] = jnp.zeros(acc.shape, F32)
        own = id_of(sc, t, step)

        def per_key(j, _):
            @pl.when(id_of(sc, j, step) <= own)
            def _():
                def scores_of(r, n):
                    return lax.dot_general(
                        qs[t, r : r + BLOCK], ks[j, n : n + chunk, :], (((1,), (1,)), ((), ())),
                        preferred_element_type=F32,
                    )

                todo = [(r, n) for r in range(0, QROWS, BLOCK) for n in range(0, keys, chunk)]
                ahead = scores_of(*todo[0])
                for x, (r, n) in enumerate(todo):
                    scores = ahead
                    rows = slice(r, r + BLOCK)
                    if n == 0:
                        old, total = top[rows], acc[rows]
                    if x + 1 < len(todo):
                        ahead = scores_of(*todo[x + 1])
                    new = jnp.maximum(old, jnp.max(scores, axis=-1, keepdims=True))
                    weights = jnp.exp2(scores - new[:, :1]).astype(BF)
                    shrink = jnp.exp2(old - new)
                    total = total * jnp.concatenate([shrink, shrink], axis=1) + jnp.dot(
                        weights, vs[j, n : n + chunk, :], preferred_element_type=F32
                    )
                    old = new
                    if n + chunk == keys:
                        top[rows] = new
                        acc[rows] = total

            return 0

        lax.fori_loop(0, SLOTS, per_key, 0)
        if last:
            res = (acc[:, :HD] / acc[:, HD:]).astype(BF)
            rows = pl.ds(pl.multiple_of(t * HALF, HALF), HALF)
            for c in range(4):
                for m in range(3):
                    piece = res[(c * 3 + m) * HALF : (c * 3 + m + 1) * HALF]
                    out[c, m, rows, :] = piece
                    out[4 + c, m, rows, :] = piece
        return 0

    lax.fori_loop(0, SLOTS, per_span, 0)


def attend(step, sc, q, blocks, chunk, state=None):
    last = state is not None
    keys = sum(b.shape[0] for b in blocks) * HALF

    def body(*refs):
        attend_body(step, len(blocks), chunk, last, *refs)

    state_shapes = [(QROWS, HD), (QROWS, 2 * HD)]
    scratch = [
        pltpu.VMEM((SLOTS, QROWS, HD), BF),
        pltpu.VMEM((SLOTS, keys, HD), BF),
        pltpu.VMEM((SLOTS, keys, 2 * HD), BF),
    ]
    if last:
        out_shape = jax.ShapeDtypeStruct((8, 3, ROWS, HD), BF)
        scratch += [pltpu.VMEM(x, F32) for x in state_shapes]
    else:
        out_shape = [jax.ShapeDtypeStruct((SLOTS, *x), F32) for x in state_shapes]
    pairs = 10 * QROWS * keys
    return pl.pallas_call(
        body,
        in_specs=[SM] + [VM] * (1 + len(blocks) + (2 if last else 0)),
        out_specs=VM if last else [VM, VM],
        out_shape=out_shape,
        scratch_shapes=scratch,
        compiler_params=params(32),
        cost_estimate=pl.CostEstimate(
            flops=pairs * HD * 8, bytes_accessed=8 * 10**6, transcendentals=pairs
        ),
        name="span_attention_end" if last else "span_attention_begin",
    )(sc, q, *blocks, *(state or ()))


def out_body(step, sc, mine, other, ada, w, out, attn):
    n = pl.program_id(0)
    s = sc[8]
    i = s % 2
    width = w.shape[1]

    @pl.when(n == 0)
    def _():
        for m in range(24):
            attn[:ROWS, m * HD : (m + 1) * HD] = mine[m]
            attn[ROWS:, m * HD : (m + 1) * HD] = other[m]

    product = jnp.dot(attn[...], w[...], preferred_element_type=F32)
    cols = pl.ds(pl.multiple_of(s * COLS + n * width, 128), width)
    for t in range(SLOTS):
        gate = ada[level_of(sc, t, step), 2:3, cols]
        for a in range(2):
            at = (a * SLOTS + t) * HALF
            piece = (product[at : at + HALF] * gate).astype(BF)
            if step == 0:
                out[at : at + HALF, :] = piece
            else:
                rows = pl.ds(pl.multiple_of((i ^ a) * HALF, HALF), HALF)
                out[s ^ t, rows, :] = piece


def out_projection(step, sc, mine, other, ada, w):
    width = 256
    if step == 0:
        out_spec = pl.BlockSpec((2 * ROWS, width), lambda n: (0, n))
        out_shape = jax.ShapeDtypeStruct((2 * ROWS, COLS), BF)
    else:
        out_spec = pl.BlockSpec((SLOTS, TOK, width), lambda n: (0, 0, n))
        out_shape = jax.ShapeDtypeStruct((SLOTS, TOK, COLS), BF)

    def body(*refs):
        out_body(step, *refs)

    return pl.pallas_call(
        body,
        grid=(COLS // width,),
        in_specs=[SM]
        + [whole((24, ROWS, HD))] * 2
        + [whole(ada.shape), pl.BlockSpec((WIDTH, width), lambda n: (0, n))],
        out_specs=out_spec,
        out_shape=out_shape,
        scratch_shapes=[pltpu.VMEM((2 * ROWS, WIDTH), BF)],
        compiler_params=params(32),
        name="out_projection",
    )(sc, mine, other, ada, w)


def finish_body(sc, vel, r0, r1, r2, r3, out):
    s = sc[8]
    out[0] = vel[...]
    for k, r in enumerate((r0, r1, r2, r3)):
        out[1, :, col_of(s ^ k)] = r[...]


def finish(sc, vel, rs):
    return pl.pallas_call(
        finish_body,
        in_specs=[SM] + [VM] * 5,
        out_specs=VM,
        out_shape=jax.ShapeDtypeStruct((2, TOK, WIDTH), BF),
        compiler_params=params(16),
        name="collect_velocity",
    )(sc, vel, *rs)


def gather_slots(x):
    far = move(x, h=1)
    near = move(x, i=1)
    return x, near, far, move(far, i=1)


def gather_keys(low, high):
    low_y = move(low, y=2)
    high_z = [move(high, z=k) for k in (1, -1, 2)]
    early = jnp.concatenate([low, high, low_y, *high_z])
    lows = jnp.concatenate([low, low_y])
    highs = jnp.concatenate([high, *high_z])
    late = [move(lows, z=k) for k in (1, -1, 2)] + [move(highs, y=2)]
    late = jnp.concatenate(late)
    return [early, move(early, i=1)], [late, move(late, i=1)]


def shards(latents, fresh, span_ids, noise_step, ada_table, w_qkv, w_out):
    pos = lax.axis_index("slot").astype(jnp.int32).reshape(1)
    sc = jnp.concatenate([span_ids, noise_step, pos])
    own = latents[0]

    def one_step(step, *parts):
        got = exchange(pack(sc, *parts))
        early, late = gather_keys(got[4:6, 3:], got[6:, 3:])
        state = attend(step, sc, got, early, 768)
        attn = attend(step, sc, got, late, 1280, state)
        attn = exchange(attn).reshape(24, ROWS, HD)
        return out_projection(step, sc, attn, move(attn, i=1), ada_table, w_out)

    xs = gather_slots(own)
    mine_a, theirs_a = first_projection(sc, xs[:2], 0, ada_table, w_qkv)
    other_a = move(theirs_a, i=1)
    mine_b, theirs_b = first_projection(sc, xs[2:], 2, ada_table, w_qkv)
    vel = one_step(0, mine_a, mine_b, other_a, move(theirs_b, i=1))
    mine, theirs, vel, fin = second_projection(sc, xs, gather_slots(vel), fresh, ada_table, w_qkv)
    out = one_step(1, mine, move(theirs, i=1))
    rs = [out[0], move(out[1], i=1), move(out[2], h=1), move(out[3], h=1, i=1)]
    return finish(sc, vel, rs)[:, None], fin


def solution(mesh):
    in_specs = (
        P("slot", "ctx", None),
        P("ctx", None),
        P(),
        P(),
        P(),
        P(None, "slot"),
        P(None, "slot"),
    )
    out_specs = (P(None, "slot", "ctx", None), P("ctx", "slot"))
    return jax.shard_map(shards, mesh=mesh, in_specs=in_specs, out_specs=out_specs, check_vma=False)
```

time: 261 us -> 256 us (0.981)
  blocking collectives: 84.4 us -> 70.3 us
  Pallas kernels: 59.6 us -> 66.4 us
  local copies, waits for them, and re-layouts: 9.52 us -> 5.86 us
  waiting for transfers between devices: 56.1 us -> 59.4 us
    all_to_all x6 -> x4, blocking collectives: 84.4 us -> 70.3 us  [exchange(): lax.all_to_all(x, AXES, 0, 0, tiled=True, axis_index_groups=group_lists())]
    pallas_call x8 -> x11, Pallas kernels: 58.7 us -> 64.9 us  [the longest x4 43 us: attend(): pl.pallas_call(body, in_specs=[SM] + [VM] * (1 + len(blocks) + (2 if last...]
    unnamed x44 -> x36, local copies, waits for them, and re-layouts: 9.27 us -> 5.61 us
    ppermute x33 -> x34, waiting for transfers between devices: 56.1 us -> 59.4 us  [move(): return lax.ppermute(x, AXES, pairs)]
    ppermute x33 -> x34, starting transfers between devices: 49.9 us -> 52.1 us  [move(): return lax.ppermute(x, AXES, pairs)]
  transfers between devices with their start and end apart: 33 -> 34, of which waited for: 20 -> 21; matrix products, arithmetic and copies ran while one was open for 0% -> 1% of each run, Pallas kernels for 0% -> 10%
where the time goes in v2:
time: 256 us
  blocking collectives  70.3 us (27%)
  Pallas kernels  66.4 us (26%)
  waiting for transfers between devices  59.4 us (23%)
  starting transfers between devices  52.1 us (20%)
  local copies, waits for them, and re-layouts  5.86 us (2%)
    all_to_all x4, blocking collectives, exchange(): lax.all_to_all(x, AXES, 0, 0, tiled=True, axis_index_groups=group_lists())  70.3 us
    ppermute x34, waiting for transfers between devices, move(): return lax.ppermute(x, AXES, pairs)  59.4 us
    ppermute x34, starting transfers between devices, move(): return lax.ppermute(x, AXES, pairs)  52.1 us
    pallas_call x4, Pallas kernels, attend(): pl.pallas_call(body, in_specs=[SM] + [VM] * (1 + len(blocks) + (2 if last...  43 us
    pallas_call x1, Pallas kernels, second_projection(): pl.pallas_call(second_body, grid=(heads // 2,), in_specs=[SM] + [whole((T...  7.2 us
    pallas_call x2, Pallas kernels, first_projection(): pl.pallas_call(body, grid=(heads // 2,), in_specs=[SM] + [whole((TOK, WID...  7.19 us
    pallas_call x2, Pallas kernels, out_projection(): pl.pallas_call(body, grid=(COLS // width,), in_specs=[SM] + [whole((24, R...  6.06 us
    unnamed x36, local copies, waits for them, and re-layouts  5.61 us
  transfers between devices with their start and end apart: 34, of which 21 were waited for; matrix products, arithmetic and copies ran while one was open for 1% of the time, Pallas kernels for 10%

profile of v2, /device:TPU:1, one launch (start us, length us, event | category | flops | bytes accessed | tf_op | source)
XLA Modules:
  0.0 255.8 jit_solution(6078945408024304247)
XLA Ops:
  0.6 3.7 %collective-permute-start.1 = (bf16[64,3072]{1,0:T(8,128)(2,1)}, bf16[64,3072]{1,0:T(8,128)(2,1)S(1)}, u32[]{:S(2)}, u32[]{:S(2)}) collective-permute-start(bf16[64,3072]{1,0:T(8,128)(2,1)} %bitcast.23), channel_id=1, source_target_pairs={{0,64},{1,65},{2,66},{3,67},{4,68},{5,69},{6,70},{7,71},{8,72},{9,... | collective-permute-start | bytes 1179656 | tf_op jit(solution)/shard_map/ppermute | solution.py:45
  5.2 7.6 %collective-permute-done.1.refs_1_.x2 = bf16[64,3072]{1,0:T(8,128)(2,1)S(1)} collective-permute-done((bf16[64,3072]{1,0:T(8,128)(2,1)}, bf16[64,3072]{1,0:T(8,128)(2,1)S(1)}, u32[]{:S(2)}, u32[]{:S(2)}) %collective-permute-start.1) | collective-permute-done | bytes 393248 | tf_op jit(solution)/shard_map/ppermute | solution.py:45
  15.3 3.2 %copy-done = bf16[3072,1280]{1,0:T(8,128)(2,1)S(1)} copy-done((bf16[3072,1280]{1,0:T(8,128)(2,1)S(1)}, bf16[3072,1280]{1,0:T(8,128)(2,1)}, u32[]{:S(2)}) %copy-start) | copy-done | bytes 7864344
  20.6 3.6 %modulate_project.2 = (bf16[10,64,128]{2,1,0:T(8,128)(2,1)S(1)}, bf16[10,64,128]{2,1,0:T(8,128)(2,1)S(1)}) custom-call(s32[9]{0:T(128)S(1)} %pad_add_fusion.refs_0_.sc, bf16[64,3072]{1,0:T(8,128)(2,1)S(1)} %bitcast.25, bf16[64,3072]{1,0:T(8,128)(2,1)S(1)} %collective-permute-done.refs_2_.x1, f32[9,3,3072]{2,1,0:T(4,128)S(1)} %copy-done.2, ...), custom_call_target="tpu_custom_call" | custom-call | flops 4000000000 | bytes 10000000 | tf_op jit(solution)/shard_map/modulate_project/pallas_call | solution.py:191
  24.3 3.6 %modulate_project.3 = (bf16[10,64,128]{2,1,0:T(8,128)(2,1)S(1)}, bf16[10,64,128]{2,1,0:T(8,128)(2,1)S(1)}) custom-call(s32[9]{0:T(128)S(1)} %pad_add_fusion.refs_0_.sc, bf16[64,3072]{1,0:T(8,128)(2,1)S(1)} %collective-permute-done.1.refs_1_.x2, bf16[64,3072]{1,0:T(8,128)(2,1)S(1)} %collective-permute-done.2.refs_2_.x3, f32[9,3,3072]{2,1,0:T(4,128)S(1)} %copy-done.2, ...), custom_call_target="tpu_custom_call" | custom-call | flops 4000000000 | bytes 10000000 | tf_op jit(solution)/shard_map/modulate_project/pallas_call | solution.py:191
  30.2 22.1 %all_to_all.20.refs_1_ = bf16[8,5,128,128]{3,2,1,0:T(8,128)(2,1)S(1)} all-to-all(bf16[8,5,128,128]{3,2,1,0:T(8,128)(2,1)S(1)} %pack_heads.2), channel_id=1, replica_groups={{0,1,4,5,64,65,68,69},{2,3,6,7,66,67,70,71},{8,9,12,13,72,73,76,77},{10..., dimensions={0} | all-to-all | bytes 2621440 | tf_op jit(solution)/shard_map/all_to_all | solution.py:65
  55.0 3.6 %collective-permute-start.11 = (bf16[2,2,128,128]{3,2,1,0:T(8,128)(2,1)S(1)}, bf16[2,2,128,128]{3,2,1,0:T(8,128)(2,1)S(1)}, u32[]{:S(2)}, u32[]{:S(2)}) collective-permute-start(bf16[2,2,128,128]{3,2,1,0:T(8,128)(2,1)S(1)} %get-tuple-element.30), channel_id=1, source_target_pairs={{0,16},{1,17},{2,18},{3,19},{4,20},{5,21},{6,22},{7,23},{8,24},{9,... | collective-permute-start | bytes 393224 | tf_op jit(solution)/shard_map/ppermute | solution.py:45
  66.3 3.9 %collective-permute-done.6 = bf16[4,2,128,128]{3,2,1,0:T(8,128)(2,1)S(1)} collective-permute-done((bf16[4,2,128,128]{3,2,1,0:T(8,128)(2,1)S(1)}, bf16[4,2,128,128]{3,2,1,0:T(8,128)(2,1)S(1)}, u32[]{:S(2)}, u32[]{:S(2)}) %collective-permute-start.6) | collective-permute-done | bytes 262176 | tf_op jit(solution)/shard_map/ppermute | solution.py:45
  70.2 4.8 %collective-permute-done.8 = bf16[4,2,128,128]{3,2,1,0:T(8,128)(2,1)S(1)} collective-permute-done((bf16[4,2,128,128]{3,2,1,0:T(8,128)(2,1)S(1)}, bf16[4,2,128,128]{3,2,1,0:T(8,128)(2,1)S(1)}, u32[]{:S(2)}, u32[]{:S(2)}) %collective-permute-start.8) | collective-permute-done | bytes 262176 | tf_op jit(solution)/shard_map/ppermute | solution.py:45
  76.0 5.3 %collective-permute-start.13 = (bf16[20,2,128,128]{3,2,1,0:T(8,128)(2,1)S(1)}, bf16[20,2,128,128]{3,2,1,0:T(8,128)(2,1)S(1)}, u32[]{:S(2)}, u32[]{:S(2)}) collective-permute-start(bf16[20,2,128,128]{3,2,1,0:T(8,128)(2,1)S(1)} %constant_dynamic-update-slice_fusion.refs_2_), channel_id=1, source_target_pairs={{0,32},{1,33},{2,34},{3,35},{4,36},{5,37},{6,38},{7,39},{8,40},{9,... | collective-permute-start | bytes 3932168 | tf_op jit(solution)/shard_map/ppermute | solution.py:45
  81.5 3.6 %collective-permute-done.14.refs_3_ = bf16[12,2,128,128]{3,2,1,0:T(8,128)(2,1)S(1)} collective-permute-done((bf16[12,2,128,128]{3,2,1,0:T(8,128)(2,1)S(1)}, bf16[12,2,128,128]{3,2,1,0:T(8,128)(2,1)S(1)}, u32[]{:S(2)}, u32[]{:S(2)}) %collective-permute-start.14) | collective-permute-done | bytes 786464 | tf_op jit(solution)/shard_map/ppermute | solution.py:45
  85.1 9.6 %span_attention_begin.2 = (f32[4,384,128]{2,1,0:T(8,128)S(1)}, f32[4,384,256]{2,1,0:T(8,128)S(1)}) custom-call(s32[9]{0:T(128)S(1)} %pad_add_fusion.refs_0_.sc, bf16[8,5,128,128]{3,2,1,0:T(8,128)(2,1)S(1)} %all_to_all.20.refs_1_, bf16[12,2,128,128]{3,2,1,0:T(8,128)(2,1)S(1)} %constant_dynamic-update-slice_fusion.4.refs_2_, ...), custom_call_target="tpu_custom_call" | custom-call | flops 3019898880 | bytes 8000000 | tf_op jit(solution)/shard_map/span_attention_begin/pallas_call | solution.py:374
  94.8 11.8 %span_attention_end.2 = bf16[8,3,128,128]{3,2,1,0:T(8,128)(2,1)S(1)} custom-call(s32[9]{0:T(128)S(1)} %pad_add_fusion.refs_0_.sc, bf16[8,5,128,128]{3,2,1,0:T(8,128)(2,1)S(1)} %all_to_all.20.refs_1_, bf16[20,2,128,128]{3,2,1,0:T(8,128)(2,1)S(1)} %constant_dynamic-update-slice_fusion.refs_2_, bf16[20,2,128,128]{3,2,1,0:T(8,128)(2,1)S(1)} %collective-permute-done.13.refs_3_, ...), custom_call_target="tpu_custom_call" | custom-call | flops 5033164800 | bytes 8000000 | tf_op jit(solution)/shard_map/span_attention_end/pallas_call | solution.py:374
  106.6 14.2 %all_to_all.21 = bf16[8,3,128,128]{3,2,1,0:T(8,128)(2,1)S(1)} all-to-all(bf16[8,3,128,128]{3,2,1,0:T(8,128)(2,1)S(1)} %span_attention_end.2), channel_id=1, replica_groups={{0,1,4,5,64,65,68,69},{2,3,6,7,66,67,70,71},{8,9,12,13,72,73,76,77},{10..., dimensions={0} | all-to-all | bytes 1572864 | tf_op jit(solution)/shard_map/all_to_all | solution.py:65
  129.8 10.0 %collective-permute-done.17.v2 = bf16[256,768]{1,0:T(8,128)(2,1)S(1)} collective-permute-done((bf16[256,768]{1,0:T(8,128)(2,1)S(1)}, bf16[256,768]{1,0:T(8,128)(2,1)S(1)}, u32[]{:S(2)}, u32[]{:S(2)}) %collective-permute-start.17) | collective-permute-done | bytes 393248 | tf_op jit(solution)/shard_map/ppermute | solution.py:45
  142.3 7.2 %advance_modulate_project.1 = (bf16[10,128,128]{2,1,0:T(8,128)(2,1)S(1)}, bf16[10,128,128]{2,1,0:T(8,128)(2,1)S(1)}, bf16[64,3072]{1,0:T(8,128)(2,1)S(1)}, bf16[64,768]{1,0:T(8,128)(2,1)}) custom-call(s32[9]{0:T(128)S(1)} %pad_add_fusion.refs_0_.sc, bf16[64,3072]{1,0:T(8,128)(2,1)S(1)} %bitcast.26, bf16[64,3072]{1,0:T(8,128)(2,1)S(1)} %collective-permute-done.refs_2_.x1, ...), custom_call_target="tpu_custom_call" | custom-call | tf_op jit(solution)/shard_map/advance_modulate_project/pallas_call | solution.py:208
  151.9 19.7 %all_to_all.22.refs_1_ = bf16[8,5,128,128]{3,2,1,0:T(8,128)(2,1)S(1)} all-to-all(bf16[8,5,128,128]{3,2,1,0:T(8,128)(2,1)S(1)} %pack_heads.3), channel_id=1, replica_groups={{0,1,4,5,64,65,68,69},{2,3,6,7,66,67,70,71},{8,9,12,13,72,73,76,77},{10..., dimensions={0} | all-to-all | bytes 2621440 | tf_op jit(solution)/shard_map/all_to_all | solution.py:65
  177.5 3.1 %collective-permute-start.22 = (bf16[4,2,128,128]{3,2,1,0:T(8,128)(2,1)S(1)}, bf16[4,2,128,128]{3,2,1,0:T(8,128)(2,1)S(1)}, u32[]{:S(2)}, u32[]{:S(2)}) collective-permute-start(bf16[4,2,128,128]{3,2,1,0:T(8,128)(2,1)S(1)} %pad_maximum_fusion.3), channel_id=1, source_target_pairs={{0,24},{1,25},{2,26},{3,27},{4,28},{5,29},{6,30},{7,31},{8,0},{9,1... | collective-permute-start | bytes 786440 | tf_op jit(solution)/shard_map/ppermute | solution.py:45
  187.8 5.2 %collective-permute-done.23 = bf16[4,2,128,128]{3,2,1,0:T(8,128)(2,1)S(1)} collective-permute-done((bf16[4,2,128,128]{3,2,1,0:T(8,128)(2,1)S(1)}, bf16[4,2,128,128]{3,2,1,0:T(8,128)(2,1)S(1)}, u32[]{:S(2)}, u32[]{:S(2)}) %collective-permute-start.23) | collective-permute-done | bytes 262176 | tf_op jit(solution)/shard_map/ppermute | solution.py:45
  193.6 5.5 %collective-permute-start.28 = (bf16[20,2,128,128]{3,2,1,0:T(8,128)(2,1)S(1)}, bf16[20,2,128,128]{3,2,1,0:T(8,128)(2,1)S(1)}, u32[]{:S(2)}, u32[]{:S(2)}) collective-permute-start(bf16[20,2,128,128]{3,2,1,0:T(8,128)(2,1)S(1)} %constant_dynamic-update-slice_fusion.8.refs_2_), channel_id=1, source_target_pairs={{0,32},{1,33},{2,34},{3,35},{4,36},{5,37},{6,38},{7,39},{8,40},{9,... | collective-permute-start | bytes 3932168 | tf_op jit(solution)/shard_map/ppermute | solution.py:45
  199.3 3.6 %collective-permute-done.29.refs_3_ = bf16[12,2,128,128]{3,2,1,0:T(8,128)(2,1)S(1)} collective-permute-done((bf16[12,2,128,128]{3,2,1,0:T(8,128)(2,1)S(1)}, bf16[12,2,128,128]{3,2,1,0:T(8,128)(2,1)S(1)}, u32[]{:S(2)}, u32[]{:S(2)}) %collective-permute-start.29) | collective-permute-done | bytes 786464 | tf_op jit(solution)/shard_map/ppermute | solution.py:45
  202.9 9.8 %span_attention_begin.3 = (f32[4,384,128]{2,1,0:T(8,128)S(1)}, f32[4,384,256]{2,1,0:T(8,128)S(1)}) custom-call(s32[9]{0:T(128)S(1)} %pad_add_fusion.refs_0_.sc, bf16[8,5,128,128]{3,2,1,0:T(8,128)(2,1)S(1)} %all_to_all.22.refs_1_, bf16[12,2,128,128]{3,2,1,0:T(8,128)(2,1)S(1)} %constant_dynamic-update-slice_fusion.12.refs_2_, ...), custom_call_target="tpu_custom_call" | custom-call | flops 3019898880 | bytes 8000000 | tf_op jit(solution)/shard_map/span_attention_begin/pallas_call | solution.py:374
  212.7 11.9 %span_attention_end.3 = bf16[8,3,128,128]{3,2,1,0:T(8,128)(2,1)S(1)} custom-call(s32[9]{0:T(128)S(1)} %pad_add_fusion.refs_0_.sc, bf16[8,5,128,128]{3,2,1,0:T(8,128)(2,1)S(1)} %all_to_all.22.refs_1_, bf16[20,2,128,128]{3,2,1,0:T(8,128)(2,1)S(1)} %constant_dynamic-update-slice_fusion.8.refs_2_, bf16[20,2,128,128]{3,2,1,0:T(8,128)(2,1)S(1)} %collective-permute-done.28.refs_3_, ...), custom_call_target="tpu_custom_call" | custom-call | flops 5033164800 | bytes 8000000 | tf_op jit(solution)/shard_map/span_attention_end/pallas_call | solution.py:374
  224.6 14.3 %all_to_all.23 = bf16[8,3,128,128]{3,2,1,0:T(8,128)(2,1)S(1)} all-to-all(bf16[8,3,128,128]{3,2,1,0:T(8,128)(2,1)S(1)} %span_attention_end.3), channel_id=1, replica_groups={{0,1,4,5,64,65,68,69},{2,3,6,7,66,67,70,71},{8,9,12,13,72,73,76,77},{10..., dimensions={0} | all-to-all | bytes 1572864 | tf_op jit(solution)/shard_map/all_to_all | solution.py:65
  (110 shorter events, 63.9 us)
Async XLA Ops:
  0.6 12.2 %collective-permute-start.1 = (bf16[64,3072]{1,0:T(8,128)(2,1)}, bf16[64,3072]{1,0:T(8,128)(2,1)S(1)}, u32[]{:S(2)}, u32[]{:S(2)}) collective-permute-start(bf16[64,3072]{1,0:T(8,128)(2,1)} %bitcast.23), channel_id=1, source_target_pairs={{0,64},{1,65},{2,66},{3,67},{4,68},{5,69},{6,70},{7,71},{8,72},{9,... | collective-permute-start | bytes 1179656 | tf_op jit(solution)/shard_map/ppermute | solution.py:45
  4.3 11.0 %collective-permute-start = (bf16[64,3072]{1,0:T(8,128)(2,1)}, bf16[64,3072]{1,0:T(8,128)(2,1)S(1)}, u32[]{:S(2)}, u32[]{:S(2)}) collective-permute-start(bf16[64,3072]{1,0:T(8,128)(2,1)} %bitcast.24), channel_id=1, source_target_pairs={{0,32},{1,33},{2,34},{3,35},{4,36},{5,37},{6,38},{7,39},{8,40},{9,... | collective-permute-start | bytes 1179656 | tf_op jit(solution)/shard_map/ppermute | solution.py:45
  12.9 11.4 %collective-permute-start.2 = (bf16[64,3072]{1,0:T(8,128)(2,1)S(1)}, bf16[64,3072]{1,0:T(8,128)(2,1)S(1)}, u32[]{:S(2)}, u32[]{:S(2)}) collective-permute-start(bf16[64,3072]{1,0:T(8,128)(2,1)S(1)} %collective-permute-done.1.refs_1_.x2), channel_id=1, source_target_pairs={{0,32},{1,33},{2,34},{3,35},{4,36},{5,37},{6,38},{7,39},{8,40},{9,... | collective-permute-start | bytes 1179656 | tf_op jit(solution)/shard_map/ppermute | solution.py:45
  52.3 7.8 %collective-permute-start.5 = (bf16[2,2,128,128]{3,2,1,0:T(8,128)(2,1)S(1)}, bf16[2,2,128,128]{3,2,1,0:T(8,128)(2,1)S(1)}, u32[]{:S(2)}, u32[]{:S(2)}) collective-permute-start(bf16[2,2,128,128]{3,2,1,0:T(8,128)(2,1)S(1)} %get-tuple-element.31), channel_id=1, source_target_pairs={{0,2},{1,3},{2,0},{3,1},{4,6},{5,7},{6,4},{7,5},{8,10},{9,11},{10,... | collective-permute-start | bytes 393224 | tf_op jit(solution)/shard_map/ppermute | solution.py:45
  55.0 6.8 %collective-permute-start.11 = (bf16[2,2,128,128]{3,2,1,0:T(8,128)(2,1)S(1)}, bf16[2,2,128,128]{3,2,1,0:T(8,128)(2,1)S(1)}, u32[]{:S(2)}, u32[]{:S(2)}) collective-permute-start(bf16[2,2,128,128]{3,2,1,0:T(8,128)(2,1)S(1)} %get-tuple-element.30), channel_id=1, source_target_pairs={{0,16},{1,17},{2,18},{3,19},{4,20},{5,21},{6,22},{7,23},{8,24},{9,... | collective-permute-start | bytes 393224 | tf_op jit(solution)/shard_map/ppermute | solution.py:45
  59.0 6.1 %collective-permute-start.9 = (bf16[2,2,128,128]{3,2,1,0:T(8,128)(2,1)S(1)}, bf16[2,2,128,128]{3,2,1,0:T(8,128)(2,1)S(1)}, u32[]{:S(2)}, u32[]{:S(2)}) collective-permute-start(bf16[2,2,128,128]{3,2,1,0:T(8,128)(2,1)S(1)} %get-tuple-element.30), channel_id=1, source_target_pairs={{0,8},{1,9},{2,10},{3,11},{4,12},{5,13},{6,14},{7,15},{8,16},{9,17... | collective-permute-start | bytes 393224 | tf_op jit(solution)/shard_map/ppermute | solution.py:45
  60.1 10.1 %collective-permute-start.7 = (bf16[4,2,128,128]{3,2,1,0:T(8,128)(2,1)S(1)}, bf16[4,2,128,128]{3,2,1,0:T(8,128)(2,1)S(1)}, u32[]{:S(2)}, u32[]{:S(2)}) collective-permute-start(bf16[4,2,128,128]{3,2,1,0:T(8,128)(2,1)S(1)} %pad_maximum_fusion.2), channel_id=1, source_target_pairs={{0,24},{1,25},{2,26},{3,27},{4,28},{5,29},{6,30},{7,31},{8,0},{9,1... | collective-permute-start | bytes 786440 | tf_op jit(solution)/shard_map/ppermute | solution.py:45
  61.8 8.3 %collective-permute-start.6 = (bf16[4,2,128,128]{3,2,1,0:T(8,128)(2,1)S(1)}, bf16[4,2,128,128]{3,2,1,0:T(8,128)(2,1)S(1)}, u32[]{:S(2)}, u32[]{:S(2)}) collective-permute-start(bf16[4,2,128,128]{3,2,1,0:T(8,128)(2,1)S(1)} %pad_maximum_fusion.2), channel_id=1, source_target_pairs={{0,8},{1,9},{2,10},{3,11},{4,12},{5,13},{6,14},{7,15},{8,16},{9,17... | collective-permute-start | bytes 786440 | tf_op jit(solution)/shard_map/ppermute | solution.py:45
  65.3 10.7 %collective-permute-start.12 = (bf16[8,2,128,128]{3,2,1,0:T(8,128)(2,1)S(1)}, bf16[8,2,128,128]{3,2,1,0:T(8,128)(2,1)S(1)}, u32[]{:S(2)}, u32[]{:S(2)}) collective-permute-start(bf16[8,2,128,128]{3,2,1,0:T(8,128)(2,1)S(1)} %pad_maximum_fusion), channel_id=1, source_target_pairs={{0,2},{1,3},{2,0},{3,1},{4,6},{5,7},{6,4},{7,5},{8,10},{9,11},{10,... | collective-permute-start | bytes 1572872 | tf_op jit(solution)/shard_map/ppermute | solution.py:45
  65.7 9.4 %collective-permute-start.8 = (bf16[4,2,128,128]{3,2,1,0:T(8,128)(2,1)S(1)}, bf16[4,2,128,128]{3,2,1,0:T(8,128)(2,1)S(1)}, u32[]{:S(2)}, u32[]{:S(2)}) collective-permute-start(bf16[4,2,128,128]{3,2,1,0:T(8,128)(2,1)S(1)} %pad_maximum_fusion.2), channel_id=1, source_target_pairs={{0,16},{1,17},{2,18},{3,19},{4,20},{5,21},{6,22},{7,23},{8,24},{9,... | collective-permute-start | bytes 786440 | tf_op jit(solution)/shard_map/ppermute | solution.py:45
  76.0 18.7 %collective-permute-start.13 = (bf16[20,2,128,128]{3,2,1,0:T(8,128)(2,1)S(1)}, bf16[20,2,128,128]{3,2,1,0:T(8,128)(2,1)S(1)}, u32[]{:S(2)}, u32[]{:S(2)}) collective-permute-start(bf16[20,2,128,128]{3,2,1,0:T(8,128)(2,1)S(1)} %constant_dynamic-update-slice_fusion.refs_2_), channel_id=1, source_target_pairs={{0,32},{1,33},{2,34},{3,35},{4,36},{5,37},{6,38},{7,39},{8,40},{9,... | collective-permute-start | bytes 3932168 | tf_op jit(solution)/shard_map/ppermute | solution.py:45
  127.8 11.9 %collective-permute-start.17 = (bf16[256,768]{1,0:T(8,128)(2,1)S(1)}, bf16[256,768]{1,0:T(8,128)(2,1)S(1)}, u32[]{:S(2)}, u32[]{:S(2)}) collective-permute-start(bf16[256,768]{1,0:T(8,128)(2,1)S(1)} %out_projection.2.v0), channel_id=1, source_target_pairs={{0,64},{1,65},{2,66},{3,67},{4,68},{5,69},{6,70},{7,71},{8,72},{9,... | collective-permute-start | bytes 1179656 | tf_op jit(solution)/shard_map/ppermute | solution.py:45
  129.1 11.9 %collective-permute-start.16 = (bf16[256,768]{1,0:T(8,128)(2,1)S(1)}, bf16[256,768]{1,0:T(8,128)(2,1)S(1)}, u32[]{:S(2)}, u32[]{:S(2)}) collective-permute-start(bf16[256,768]{1,0:T(8,128)(2,1)S(1)} %out_projection.2.v0), channel_id=1, source_target_pairs={{0,32},{1,33},{2,34},{3,35},{4,36},{5,37},{6,38},{7,39},{8,40},{9,... | collective-permute-start | bytes 1179656 | tf_op jit(solution)/shard_map/ppermute | solution.py:45
  171.6 5.9 %collective-permute-start.20 = (bf16[2,2,128,128]{3,2,1,0:T(8,128)(2,1)S(1)}, bf16[2,2,128,128]{3,2,1,0:T(8,128)(2,1)S(1)}, u32[]{:S(2)}, u32[]{:S(2)}) collective-permute-start(bf16[2,2,128,128]{3,2,1,0:T(8,128)(2,1)S(1)} %get-tuple-element.29), channel_id=1, source_target_pairs={{0,2},{1,3},{2,0},{3,1},{4,6},{5,7},{6,4},{7,5},{8,10},{9,11},{10,... | collective-permute-start | bytes 393224 | tf_op jit(solution)/shard_map/ppermute | solution.py:45
  173.2 7.4 %collective-permute-start.26 = (bf16[2,2,128,128]{3,2,1,0:T(8,128)(2,1)S(1)}, bf16[2,2,128,128]{3,2,1,0:T(8,128)(2,1)S(1)}, u32[]{:S(2)}, u32[]{:S(2)}) collective-permute-start(bf16[2,2,128,128]{3,2,1,0:T(8,128)(2,1)S(1)} %get-tuple-element.28), channel_id=1, source_target_pairs={{0,16},{1,17},{2,18},{3,19},{4,20},{5,21},{6,22},{7,23},{8,24},{9,... | collective-permute-start | bytes 393224 | tf_op jit(solution)/shard_map/ppermute | solution.py:45
  176.0 5.5 %collective-permute-start.25 = (bf16[2,2,128,128]{3,2,1,0:T(8,128)(2,1)S(1)}, bf16[2,2,128,128]{3,2,1,0:T(8,128)(2,1)S(1)}, u32[]{:S(2)}, u32[]{:S(2)}) collective-permute-start(bf16[2,2,128,128]{3,2,1,0:T(8,128)(2,1)S(1)} %get-tuple-element.28), channel_id=1, source_target_pairs={{0,24},{1,25},{2,26},{3,27},{4,28},{5,29},{6,30},{7,31},{8,0},{9,1... | collective-permute-start | bytes 393224 | tf_op jit(solution)/shard_map/ppermute | solution.py:45
  176.8 6.2 %collective-permute-start.24 = (bf16[2,2,128,128]{3,2,1,0:T(8,128)(2,1)S(1)}, bf16[2,2,128,128]{3,2,1,0:T(8,128)(2,1)S(1)}, u32[]{:S(2)}, u32[]{:S(2)}) collective-permute-start(bf16[2,2,128,128]{3,2,1,0:T(8,128)(2,1)S(1)} %get-tuple-element.28), channel_id=1, source_target_pairs={{0,8},{1,9},{2,10},{3,11},{4,12},{5,13},{6,14},{7,15},{8,16},{9,17... | collective-permute-start | bytes 393224 | tf_op jit(solution)/shard_map/ppermute | solution.py:45
  177.5 10.3 %collective-permute-start.22 = (bf16[4,2,128,128]{3,2,1,0:T(8,128)(2,1)S(1)}, bf16[4,2,128,128]{3,2,1,0:T(8,128)(2,1)S(1)}, u32[]{:S(2)}, u32[]{:S(2)}) collective-permute-start(bf16[4,2,128,128]{3,2,1,0:T(8,128)(2,1)S(1)} %pad_maximum_fusion.3), channel_id=1, source_target_pairs={{0,24},{1,25},{2,26},{3,27},{4,28},{5,29},{6,30},{7,31},{8,0},{9,1... | collective-permute-start | bytes 786440 | tf_op jit(solution)/shard_map/ppermute | solution.py:45
  180.6 7.1 %collective-permute-start.21 = (bf16[4,2,128,128]{3,2,1,0:T(8,128)(2,1)S(1)}, bf16[4,2,128,128]{3,2,1,0:T(8,128)(2,1)S(1)}, u32[]{:S(2)}, u32[]{:S(2)}) collective-permute-start(bf16[4,2,128,128]{3,2,1,0:T(8,128)(2,1)S(1)} %pad_maximum_fusion.3), channel_id=1, source_target_pairs={{0,8},{1,9},{2,10},{3,11},{4,12},{5,13},{6,14},{7,15},{8,16},{9,17... | collective-permute-start | bytes 786440 | tf_op jit(solution)/shard_map/ppermute | solution.py:45
  183.0 10.5 %collective-permute-start.27 = (bf16[8,2,128,128]{3,2,1,0:T(8,128)(2,1)S(1)}, bf16[8,2,128,128]{3,2,1,0:T(8,128)(2,1)S(1)}, u32[]{:S(2)}, u32[]{:S(2)}) collective-permute-start(bf16[8,2,128,128]{3,2,1,0:T(8,128)(2,1)S(1)} %pad_maximum_fusion.1), channel_id=1, source_target_pairs={{0,2},{1,3},{2,0},{3,1},{4,6},{5,7},{6,4},{7,5},{8,10},{9,11},{10,... | collective-permute-start | bytes 1572872 | tf_op jit(solution)/shard_map/ppermute | solution.py:45
  184.5 8.5 %collective-permute-start.23 = (bf16[4,2,128,128]{3,2,1,0:T(8,128)(2,1)S(1)}, bf16[4,2,128,128]{3,2,1,0:T(8,128)(2,1)S(1)}, u32[]{:S(2)}, u32[]{:S(2)}) collective-permute-start(bf16[4,2,128,128]{3,2,1,0:T(8,128)(2,1)S(1)} %pad_maximum_fusion.3), channel_id=1, source_target_pairs={{0,16},{1,17},{2,18},{3,19},{4,20},{5,21},{6,22},{7,23},{8,24},{9,... | collective-permute-start | bytes 786440 | tf_op jit(solution)/shard_map/ppermute | solution.py:45
  193.6 19.1 %collective-permute-start.28 = (bf16[20,2,128,128]{3,2,1,0:T(8,128)(2,1)S(1)}, bf16[20,2,128,128]{3,2,1,0:T(8,128)(2,1)S(1)}, u32[]{:S(2)}, u32[]{:S(2)}) collective-permute-start(bf16[20,2,128,128]{3,2,1,0:T(8,128)(2,1)S(1)} %constant_dynamic-update-slice_fusion.8.refs_2_), channel_id=1, source_target_pairs={{0,32},{1,33},{2,34},{3,35},{4,36},{5,37},{6,38},{7,39},{8,40},{9,... | collective-permute-start | bytes 3932168 | tf_op jit(solution)/shard_map/ppermute | solution.py:45
  245.9 6.7 %collective-permute-start.33 = (bf16[64,768]{1,0:T(8,128)(2,1)S(1)}, bf16[64,768]{1,0:T(8,128)(2,1)S(1)}, u32[]{:S(2)}, u32[]{:S(2)}) collective-permute-start(bf16[64,768]{1,0:T(8,128)(2,1)S(1)} %get-tuple-element.32), channel_id=1, source_target_pairs={{0,96},{1,97},{2,98},{3,99},{4,100},{5,101},{6,102},{7,103},{8,104... | collective-permute-start | bytes 294920 | tf_op jit(solution)/shard_map/ppermute | solution.py:45
  247.4 6.9 %collective-permute-start.32 = (bf16[64,768]{1,0:T(8,128)(2,1)S(1)}, bf16[64,768]{1,0:T(8,128)(2,1)S(1)}, u32[]{:S(2)}, u32[]{:S(2)}) collective-permute-start(bf16[64,768]{1,0:T(8,128)(2,1)S(1)} %get-tuple-element.33), channel_id=1, source_target_pairs={{0,64},{1,65},{2,66},{3,67},{4,68},{5,69},{6,70},{7,71},{8,72},{9,... | collective-permute-start | bytes 294920 | tf_op jit(solution)/shard_map/ppermute | solution.py:45
  (21 other events, 270.3 us)

commit v3 on v2

--- a/solution.py
+++ b/solution.py
@@ -461,15 +461,14 @@
     return x, near, far, move(far, i=1)
 
 
-def gather_keys(low, high):
+def begin_keys(low, high):
     low_y = move(low, y=2)
     high_z = [move(high, z=k) for k in (1, -1, 2)]
     early = jnp.concatenate([low, high, low_y, *high_z])
     lows = jnp.concatenate([low, low_y])
     highs = jnp.concatenate([high, *high_z])
     late = [move(lows, z=k) for k in (1, -1, 2)] + [move(highs, y=2)]
-    late = jnp.concatenate(late)
-    return [early, move(early, i=1)], [late, move(late, i=1)]
+    return [early, move(early, i=1)], late
 
 
 def shards(latents, fresh, span_ids, noise_step, ada_table, w_qkv, w_out):
@@ -479,17 +478,24 @@
 
     def one_step(step, *parts):
         got = exchange(pack(sc, *parts))
-        early, late = gather_keys(got[4:6, 3:], got[6:, 3:])
+        early, late = begin_keys(got[4:6, 3:], got[6:, 3:])
         state = attend(step, sc, got, early, 768)
-        attn = attend(step, sc, got, late, 1280, state)
+        late, state = lax.optimization_barrier((late, state))
+        late = jnp.concatenate(late)
+        attn = attend(step, sc, got, [late, move(late, i=1)], 1280, state)
         attn = exchange(attn).reshape(24, ROWS, HD)
         return out_projection(step, sc, attn, move(attn, i=1), ada_table, w_out)
 
-    xs = gather_slots(own)
-    mine_a, theirs_a = first_projection(sc, xs[:2], 0, ada_table, w_qkv)
-    other_a = move(theirs_a, i=1)
-    mine_b, theirs_b = first_projection(sc, xs[2:], 2, ada_table, w_qkv)
-    vel = one_step(0, mine_a, mine_b, other_a, move(theirs_b, i=1))
+    far = move(own, h=1)
+    near = move(own, i=1)
+    near_parts = first_projection(sc, (own, near), 0, ada_table, w_qkv)
+    far, near_parts = lax.optimization_barrier((far, near_parts))
+    far_near = move(far, i=1)
+    far_parts = first_projection(sc, (far, far_near), 2, ada_table, w_qkv)
+    vel = one_step(
+        0, near_parts[0], far_parts[0], move(near_parts[1], i=1), move(far_parts[1], i=1)
+    )
+    xs = (own, near, far, far_near)
     mine, theirs, vel, fin = second_projection(sc, xs, gather_slots(vel), fresh, ada_table, w_qkv)
     out = one_step(1, mine, move(theirs, i=1))
     rs = [out[0], move(out[1], i=1), move(out[2], h=1), move(out[3], h=1, i=1)]

time: 256 us -> 234 us (0.914)
  waiting for transfers between devices: 59.4 us -> 41.3 us
  starting transfers between devices: 52.1 us -> 47.8 us
    ppermute x34, waiting for transfers between devices: 59.4 us -> 41.3 us  [move(): return lax.ppermute(x, AXES, pairs)]
    ppermute x34, starting transfers between devices: 52.1 us -> 47.8 us  [move(): return lax.ppermute(x, AXES, pairs)]
  transfers between devices with their start and end apart: 34 -> 34, of which waited for: 21 -> 17; matrix products, arithmetic and copies ran while one was open for 1% -> 0% of each run, Pallas kernels for 10% -> 11%
where the time goes in v3:
time: 234 us
  blocking collectives  70.4 us (30%)
  Pallas kernels  66.3 us (28%)
  starting transfers between devices  47.8 us (20%)
  waiting for transfers between devices  41.3 us (18%)
  local copies, waits for them, and re-layouts  5.88 us (3%)
    all_to_all x4, blocking collectives, exchange(): lax.all_to_all(x, AXES, 0, 0, tiled=True, axis_index_groups=group_lists())  70.4 us
    ppermute x34, starting transfers between devices, move(): return lax.ppermute(x, AXES, pairs)  47.8 us
    pallas_call x4, Pallas kernels, attend(): pl.pallas_call(body, in_specs=[SM] + [VM] * (1 + len(blocks) + (2 if last...  43 us
    ppermute x34, waiting for transfers between devices, move(): return lax.ppermute(x, AXES, pairs)  41.3 us
    pallas_call x1, Pallas kernels, second_projection(): pl.pallas_call(second_body, grid=(heads // 2,), in_specs=[SM] + [whole((T...  7.2 us
    pallas_call x2, Pallas kernels, first_projection(): pl.pallas_call(body, grid=(heads // 2,), in_specs=[SM] + [whole((TOK, WID...  7.17 us
    pallas_call x2, Pallas kernels, out_projection(): pl.pallas_call(body, grid=(COLS // width,), in_specs=[SM] + [whole((24, R...  6.06 us
    unnamed x36, local copies, waits for them, and re-layouts  5.62 us
  transfers between devices with their start and end apart: 34, of which 17 were waited for; matrix products, arithmetic and copies ran while one was open for 0% of the time, Pallas kernels for 11%

profile of v3, /device:TPU:1, one launch (start us, length us, event | category | flops | bytes accessed | tf_op | source)
XLA Modules:
  0.0 233.6 jit_solution(15608340037325871254)
XLA Ops:
  2.1 2.8 %collective-permute-start.1 = (bf16[64,3072]{1,0:T(8,128)(2,1)}, bf16[64,3072]{1,0:T(8,128)(2,1)S(1)}, u32[]{:S(2)}, u32[]{:S(2)}) collective-permute-start(bf16[64,3072]{1,0:T(8,128)(2,1)} %bitcast.24), channel_id=1, source_target_pairs={{0,64},{1,65},{2,66},{3,67},{4,68},{5,69},{6,70},{7,71},{8,72},{9,... | collective-permute-start | bytes 1179656 | tf_op jit(solution)/shard_map/ppermute | solution.py:45
  5.7 3.2 %copy-done = bf16[3072,1280]{1,0:T(8,128)(2,1)S(1)} copy-done((bf16[3072,1280]{1,0:T(8,128)(2,1)S(1)}, bf16[3072,1280]{1,0:T(8,128)(2,1)}, u32[]{:S(2)}) %copy-start) | copy-done | bytes 7864344
  11.0 3.6 %modulate_project.2 = (bf16[10,64,128]{2,1,0:T(8,128)(2,1)S(1)}, bf16[10,64,128]{2,1,0:T(8,128)(2,1)S(1)}) custom-call(s32[9]{0:T(128)S(1)} %pad_add_fusion.refs_0_.sc, bf16[64,3072]{1,0:T(8,128)(2,1)S(1)} %bitcast.25, bf16[64,3072]{1,0:T(8,128)(2,1)S(1)} %collective-permute-done.refs_2_.x1, f32[9,3,3072]{2,1,0:T(4,128)S(1)} %copy-done.2, ...), custom_call_target="tpu_custom_call" | custom-call | flops 4000000000 | bytes 10000000 | tf_op jit(solution)/shard_map/modulate_project/pallas_call | solution.py:191
  16.7 3.6 %modulate_project.3 = (bf16[10,64,128]{2,1,0:T(8,128)(2,1)S(1)}, bf16[10,64,128]{2,1,0:T(8,128)(2,1)S(1)}) custom-call(s32[9]{0:T(128)S(1)} %pad_add_fusion.refs_0_.sc, bf16[64,3072]{1,0:T(8,128)(2,1)S(1)} %collective-permute-done.1.refs_1_.x2, bf16[64,3072]{1,0:T(8,128)(2,1)S(1)} %collective-permute-done.2.refs_2_.x3, f32[9,3,3072]{2,1,0:T(4,128)S(1)} %copy-done.2, ...), custom_call_target="tpu_custom_call" | custom-call | flops 4000000000 | bytes 10000000 | tf_op jit(solution)/shard_map/modulate_project/pallas_call | solution.py:191
  22.5 22.0 %all_to_all.20.refs_1_ = bf16[8,5,128,128]{3,2,1,0:T(8,128)(2,1)S(1)} all-to-all(bf16[8,5,128,128]{3,2,1,0:T(8,128)(2,1)S(1)} %pack_heads.2), channel_id=1, replica_groups={{0,1,4,5,64,65,68,69},{2,3,6,7,66,67,70,71},{8,9,12,13,72,73,76,77},{10..., dimensions={0} | all-to-all | bytes 2621440 | tf_op jit(solution)/shard_map/all_to_all | solution.py:65
  44.5 3.7 %collective-permute-start.11 = (bf16[2,2,128,128]{3,2,1,0:T(8,128)(2,1)S(1)}, bf16[2,2,128,128]{3,2,1,0:T(8,128)(2,1)S(1)}, u32[]{:S(2)}, u32[]{:S(2)}) collective-permute-start(bf16[2,2,128,128]{3,2,1,0:T(8,128)(2,1)S(1)} %get-tuple-element.60), channel_id=1, source_target_pairs={{0,16},{1,17},{2,18},{3,19},{4,20},{5,21},{6,22},{7,23},{8,24},{9,... | collective-permute-start | bytes 393224 | tf_op jit(solution)/shard_map/ppermute | solution.py:45
  52.3 2.7 %collective-permute-done.5 = bf16[2,2,128,128]{3,2,1,0:T(8,128)(2,1)S(1)} collective-permute-done((bf16[2,2,128,128]{3,2,1,0:T(8,128)(2,1)S(1)}, bf16[2,2,128,128]{3,2,1,0:T(8,128)(2,1)S(1)}, u32[]{:S(2)}, u32[]{:S(2)}) %collective-permute-start.5) | collective-permute-done | bytes 131104 | tf_op jit(solution)/shard_map/ppermute | solution.py:45
  55.1 4.1 %collective-permute-start.13 = (bf16[12,2,128,128]{3,2,1,0:T(8,128)(2,1)S(1)}, bf16[12,2,128,128]{3,2,1,0:T(8,128)(2,1)S(1)}, u32[]{:S(2)}, u32[]{:S(2)}) collective-permute-start(bf16[12,2,128,128]{3,2,1,0:T(8,128)(2,1)S(1)} %constant_dynamic-update-slice_fusion.refs_2_), channel_id=1, source_target_pairs={{0,32},{1,33},{2,34},{3,35},{4,36},{5,37},{6,38},{7,39},{8,40},{9,... | collective-permute-start | bytes 2359304 | tf_op jit(solution)/shard_map/ppermute | solution.py:45
  59.3 2.7 %collective-permute-start.12 = (bf16[8,2,128,128]{3,2,1,0:T(8,128)(2,1)S(1)}, bf16[8,2,128,128]{3,2,1,0:T(8,128)(2,1)S(1)}, u32[]{:S(2)}, u32[]{:S(2)}) collective-permute-start(bf16[8,2,128,128]{3,2,1,0:T(8,128)(2,1)S(1)} %pad_maximum_fusion), channel_id=1, source_target_pairs={{0,2},{1,3},{2,0},{3,1},{4,6},{5,7},{6,4},{7,5},{8,10},{9,11},{10,... | collective-permute-start | bytes 1572872 | tf_op jit(solution)/shard_map/ppermute | solution.py:45
  65.3 9.6 %span_attention_begin.2 = (f32[4,384,128]{2,1,0:T(8,128)S(1)}, f32[4,384,256]{2,1,0:T(8,128)S(1)}) custom-call(s32[9]{0:T(128)S(1)} %pad_add_fusion.refs_0_.sc, bf16[8,5,128,128]{3,2,1,0:T(8,128)(2,1)S(1)} %all_to_all.20.refs_1_, bf16[12,2,128,128]{3,2,1,0:T(8,128)(2,1)S(1)} %constant_dynamic-update-slice_fusion.refs_2_, ...), custom_call_target="tpu_custom_call" | custom-call | flops 3019898880 | bytes 8000000 | tf_op jit(solution)/shard_map/span_attention_begin/pallas_call | solution.py:374
  78.3 2.7 %collective-permute-done.14.refs_3_ = bf16[20,2,128,128]{3,2,1,0:T(8,128)(2,1)S(1)} collective-permute-done((bf16[20,2,128,128]{3,2,1,0:T(8,128)(2,1)S(1)}, bf16[20,2,128,128]{3,2,1,0:T(8,128)(2,1)S(1)}, u32[]{:S(2)}, u32[]{:S(2)}) %collective-permute-start.14) | collective-permute-done | bytes 1310752 | tf_op jit(solution)/shard_map/ppermute | solution.py:45
  81.0 11.8 %span_attention_end.2 = bf16[8,3,128,128]{3,2,1,0:T(8,128)(2,1)S(1)} custom-call(s32[9]{0:T(128)S(1)} %pad_add_fusion.refs_0_.sc, bf16[8,5,128,128]{3,2,1,0:T(8,128)(2,1)S(1)} %all_to_all.20.refs_1_, bf16[20,2,128,128]{3,2,1,0:T(8,128)(2,1)S(1)} %constant_dynamic-update-slice_fusion.4.refs_2_, bf16[20,2,128,128]{3,2,1,0:T(8,128)(2,1)S(1)} %collective-permute-done.14.refs_3_, ...), custom_call_target="tpu_custom_call" | custom-call | flops 5033164800 | bytes 8000000 | tf_op jit(solution)/shard_map/span_attention_end/pallas_call | solution.py:374
  92.8 14.4 %all_to_all.21 = bf16[8,3,128,128]{3,2,1,0:T(8,128)(2,1)S(1)} all-to-all(bf16[8,3,128,128]{3,2,1,0:T(8,128)(2,1)S(1)} %span_attention_end.2), channel_id=1, replica_groups={{0,1,4,5,64,65,68,69},{2,3,6,7,66,67,70,71},{8,9,12,13,72,73,76,77},{10..., dimensions={0} | all-to-all | bytes 1572864 | tf_op jit(solution)/shard_map/all_to_all | solution.py:65
  110.7 3.0 %out_projection.2.v0 = bf16[256,768]{1,0:T(8,128)(2,1)S(1)} custom-call(s32[9]{0:T(128)S(1)} %pad_add_fusion.refs_0_.sc, bf16[24,128,128]{2,1,0:T(8,128)(2,1)S(1)} %bitcast.20, bf16[24,128,128]{2,1,0:T(8,128)(2,1)S(1)} %collective-permute-done.15.refs_2_, f32[9,3,3072]{2,1,0:T(4,128)S(1)} %copy-done.3, bf16[3072,768]{1,0:T(8,128)(2,1)S(1)} %bitcast.16), custom_call_target="tpu_custom_call" | custom-call | tf_op jit(solution)/shard_map/out_projection/pallas_call | solution.py:426
  115.7 10.0 %collective-permute-done.17.v2 = bf16[256,768]{1,0:T(8,128)(2,1)S(1)} collective-permute-done((bf16[256,768]{1,0:T(8,128)(2,1)S(1)}, bf16[256,768]{1,0:T(8,128)(2,1)S(1)}, u32[]{:S(2)}, u32[]{:S(2)}) %collective-permute-start.17) | collective-permute-done | bytes 393248 | tf_op jit(solution)/shard_map/ppermute | solution.py:45
  128.3 7.2 %advance_modulate_project.1 = (bf16[10,128,128]{2,1,0:T(8,128)(2,1)S(1)}, bf16[10,128,128]{2,1,0:T(8,128)(2,1)S(1)}, bf16[64,3072]{1,0:T(8,128)(2,1)S(1)}, bf16[64,768]{1,0:T(8,128)(2,1)}) custom-call(s32[9]{0:T(128)S(1)} %pad_add_fusion.refs_0_.sc, bf16[64,3072]{1,0:T(8,128)(2,1)S(1)} %bitcast.26, bf16[64,3072]{1,0:T(8,128)(2,1)S(1)} %collective-permute-done.refs_2_.x1, ...), custom_call_target="tpu_custom_call" | custom-call | tf_op jit(solution)/shard_map/advance_modulate_project/pallas_call | solution.py:208
  137.8 19.7 %all_to_all.22.refs_1_ = bf16[8,5,128,128]{3,2,1,0:T(8,128)(2,1)S(1)} all-to-all(bf16[8,5,128,128]{3,2,1,0:T(8,128)(2,1)S(1)} %pack_heads.3), channel_id=1, replica_groups={{0,1,4,5,64,65,68,69},{2,3,6,7,66,67,70,71},{8,9,12,13,72,73,76,77},{10..., dimensions={0} | all-to-all | bytes 2621440 | tf_op jit(solution)/shard_map/all_to_all | solution.py:65
  161.9 4.2 %collective-permute-done.20 = bf16[2,2,128,128]{3,2,1,0:T(8,128)(2,1)S(1)} collective-permute-done((bf16[2,2,128,128]{3,2,1,0:T(8,128)(2,1)S(1)}, bf16[2,2,128,128]{3,2,1,0:T(8,128)(2,1)S(1)}, u32[]{:S(2)}, u32[]{:S(2)}) %collective-permute-start.20) | collective-permute-done | bytes 131104 | tf_op jit(solution)/shard_map/ppermute | solution.py:45
  167.1 3.0 %collective-permute-start.28 = (bf16[12,2,128,128]{3,2,1,0:T(8,128)(2,1)S(1)}, bf16[12,2,128,128]{3,2,1,0:T(8,128)(2,1)S(1)}, u32[]{:S(2)}, u32[]{:S(2)}) collective-permute-start(bf16[12,2,128,128]{3,2,1,0:T(8,128)(2,1)S(1)} %constant_dynamic-update-slice_fusion.8.refs_2_), channel_id=1, source_target_pairs={{0,32},{1,33},{2,34},{3,35},{4,36},{5,37},{6,38},{7,39},{8,40},{9,... | collective-permute-start | bytes 2359304 | tf_op jit(solution)/shard_map/ppermute | solution.py:45
  175.0 9.7 %span_attention_begin.3 = (f32[4,384,128]{2,1,0:T(8,128)S(1)}, f32[4,384,256]{2,1,0:T(8,128)S(1)}) custom-call(s32[9]{0:T(128)S(1)} %pad_add_fusion.refs_0_.sc, bf16[8,5,128,128]{3,2,1,0:T(8,128)(2,1)S(1)} %all_to_all.22.refs_1_, bf16[12,2,128,128]{3,2,1,0:T(8,128)(2,1)S(1)} %constant_dynamic-update-slice_fusion.8.refs_2_, ...), custom_call_target="tpu_custom_call" | custom-call | flops 3019898880 | bytes 8000000 | tf_op jit(solution)/shard_map/span_attention_begin/pallas_call | solution.py:374
  190.9 11.9 %span_attention_end.3 = bf16[8,3,128,128]{3,2,1,0:T(8,128)(2,1)S(1)} custom-call(s32[9]{0:T(128)S(1)} %pad_add_fusion.refs_0_.sc, bf16[8,5,128,128]{3,2,1,0:T(8,128)(2,1)S(1)} %all_to_all.22.refs_1_, bf16[20,2,128,128]{3,2,1,0:T(8,128)(2,1)S(1)} %constant_dynamic-update-slice_fusion.12.refs_2_, ...), custom_call_target="tpu_custom_call" | custom-call | flops 5033164800 | bytes 8000000 | tf_op jit(solution)/shard_map/span_attention_end/pallas_call | solution.py:374
  202.7 14.3 %all_to_all.23 = bf16[8,3,128,128]{3,2,1,0:T(8,128)(2,1)S(1)} all-to-all(bf16[8,3,128,128]{3,2,1,0:T(8,128)(2,1)S(1)} %span_attention_end.3), channel_id=1, replica_groups={{0,1,4,5,64,65,68,69},{2,3,6,7,66,67,70,71},{8,9,12,13,72,73,76,77},{10..., dimensions={0} | all-to-all | bytes 1572864 | tf_op jit(solution)/shard_map/all_to_all | solution.py:65
  220.6 3.0 %out_projection.3 = bf16[4,64,768]{2,1,0:T(8,128)(2,1)S(1)} custom-call(s32[9]{0:T(128)S(1)} %pad_add_fusion.refs_0_.sc, bf16[24,128,128]{2,1,0:T(8,128)(2,1)S(1)} %bitcast.22, bf16[24,128,128]{2,1,0:T(8,128)(2,1)S(1)} %collective-permute-done.30.refs_2_, f32[9,3,3072]{2,1,0:T(4,128)S(1)} %copy-done.3, bf16[3072,768]{1,0:T(8,128)(2,1)S(1)} %bitcast.16), custom_call_target="tpu_custom_call" | custom-call | tf_op jit(solution)/shard_map/out_projection/pallas_call | solution.py:426
  227.4 2.9 %collective-permute-done.33.r3 = bf16[64,768]{1,0:T(8,128)(2,1)S(1)} collective-permute-done((bf16[64,768]{1,0:T(8,128)(2,1)S(1)}, bf16[64,768]{1,0:T(8,128)(2,1)S(1)}, u32[]{:S(2)}, u32[]{:S(2)}) %collective-permute-start.33) | collective-permute-done | bytes 98336 | tf_op jit(solution)/shard_map/ppermute | solution.py:45
  (110 shorter events, 56.7 us)
Async XLA Ops:
  2.1 12.4 %collective-permute-start.1 = (bf16[64,3072]{1,0:T(8,128)(2,1)}, bf16[64,3072]{1,0:T(8,128)(2,1)S(1)}, u32[]{:S(2)}, u32[]{:S(2)}) collective-permute-start(bf16[64,3072]{1,0:T(8,128)(2,1)} %bitcast.24), channel_id=1, source_target_pairs={{0,64},{1,65},{2,66},{3,67},{4,68},{5,69},{6,70},{7,71},{8,72},{9,... | collective-permute-start | bytes 1179656 | tf_op jit(solution)/shard_map/ppermute | solution.py:45
  15.4 5.4 %collective-permute-start.3 = (bf16[10,64,128]{2,1,0:T(8,128)(2,1)S(1)}, bf16[10,64,128]{2,1,0:T(8,128)(2,1)S(1)}, u32[]{:S(2)}, u32[]{:S(2)}) collective-permute-start(bf16[10,64,128]{2,1,0:T(8,128)(2,1)S(1)} %get-tuple-element.34), channel_id=1, source_target_pairs={{0,32},{1,33},{2,34},{3,35},{4,36},{5,37},{6,38},{7,39},{8,40},{9,... | collective-permute-start | bytes 491528 | tf_op jit(solution)/shard_map/ppermute | solution.py:45
  44.5 10.6 %collective-permute-start.11 = (bf16[2,2,128,128]{3,2,1,0:T(8,128)(2,1)S(1)}, bf16[2,2,128,128]{3,2,1,0:T(8,128)(2,1)S(1)}, u32[]{:S(2)}, u32[]{:S(2)}) collective-permute-start(bf16[2,2,128,128]{3,2,1,0:T(8,128)(2,1)S(1)} %get-tuple-element.60), channel_id=1, source_target_pairs={{0,16},{1,17},{2,18},{3,19},{4,20},{5,21},{6,22},{7,23},{8,24},{9,... | collective-permute-start | bytes 393224 | tf_op jit(solution)/shard_map/ppermute | solution.py:45
  48.2 6.9 %collective-permute-start.10 = (bf16[2,2,128,128]{3,2,1,0:T(8,128)(2,1)S(1)}, bf16[2,2,128,128]{3,2,1,0:T(8,128)(2,1)S(1)}, u32[]{:S(2)}, u32[]{:S(2)}) collective-permute-start(bf16[2,2,128,128]{3,2,1,0:T(8,128)(2,1)S(1)} %get-tuple-element.60), channel_id=1, source_target_pairs={{0,24},{1,25},{2,26},{3,27},{4,28},{5,29},{6,30},{7,31},{8,0},{9,1... | collective-permute-start | bytes 393224 | tf_op jit(solution)/shard_map/ppermute | solution.py:45
  48.6 6.4 %collective-permute-start.9 = (bf16[2,2,128,128]{3,2,1,0:T(8,128)(2,1)S(1)}, bf16[2,2,128,128]{3,2,1,0:T(8,128)(2,1)S(1)}, u32[]{:S(2)}, u32[]{:S(2)}) collective-permute-start(bf16[2,2,128,128]{3,2,1,0:T(8,128)(2,1)S(1)} %get-tuple-element.60), channel_id=1, source_target_pairs={{0,8},{1,9},{2,10},{3,11},{4,12},{5,13},{6,14},{7,15},{8,16},{9,17... | collective-permute-start | bytes 393224 | tf_op jit(solution)/shard_map/ppermute | solution.py:45
  49.7 5.3 %collective-permute-start.5 = (bf16[2,2,128,128]{3,2,1,0:T(8,128)(2,1)S(1)}, bf16[2,2,128,128]{3,2,1,0:T(8,128)(2,1)S(1)}, u32[]{:S(2)}, u32[]{:S(2)}) collective-permute-start(bf16[2,2,128,128]{3,2,1,0:T(8,128)(2,1)S(1)} %get-tuple-element.61), channel_id=1, source_target_pairs={{0,2},{1,3},{2,0},{3,1},{4,6},{5,7},{6,4},{7,5},{8,10},{9,11},{10,... | collective-permute-start | bytes 393224 | tf_op jit(solution)/shard_map/ppermute | solution.py:45
  55.1 10.1 %collective-permute-start.13 = (bf16[12,2,128,128]{3,2,1,0:T(8,128)(2,1)S(1)}, bf16[12,2,128,128]{3,2,1,0:T(8,128)(2,1)S(1)}, u32[]{:S(2)}, u32[]{:S(2)}) collective-permute-start(bf16[12,2,128,128]{3,2,1,0:T(8,128)(2,1)S(1)} %constant_dynamic-update-slice_fusion.refs_2_), channel_id=1, source_target_pairs={{0,32},{1,33},{2,34},{3,35},{4,36},{5,37},{6,38},{7,39},{8,40},{9,... | collective-permute-start | bytes 2359304 | tf_op jit(solution)/shard_map/ppermute | solution.py:45
  59.3 18.2 %collective-permute-start.12 = (bf16[8,2,128,128]{3,2,1,0:T(8,128)(2,1)S(1)}, bf16[8,2,128,128]{3,2,1,0:T(8,128)(2,1)S(1)}, u32[]{:S(2)}, u32[]{:S(2)}) collective-permute-start(bf16[8,2,128,128]{3,2,1,0:T(8,128)(2,1)S(1)} %pad_maximum_fusion), channel_id=1, source_target_pairs={{0,2},{1,3},{2,0},{3,1},{4,6},{5,7},{6,4},{7,5},{8,10},{9,11},{10,... | collective-permute-start | bytes 1572872 | tf_op jit(solution)/shard_map/ppermute | solution.py:45
  62.1 12.9 %collective-permute-start.8 = (bf16[4,2,128,128]{3,2,1,0:T(8,128)(2,1)S(1)}, bf16[4,2,128,128]{3,2,1,0:T(8,128)(2,1)S(1)}, u32[]{:S(2)}, u32[]{:S(2)}) collective-permute-start(bf16[4,2,128,128]{3,2,1,0:T(8,128)(2,1)S(1)} %pad_maximum_fusion.2), channel_id=1, source_target_pairs={{0,16},{1,17},{2,18},{3,19},{4,20},{5,21},{6,22},{7,23},{8,24},{9,... | collective-permute-start | bytes 786440 | tf_op jit(solution)/shard_map/ppermute | solution.py:45
  62.9 13.2 %collective-permute-start.7 = (bf16[4,2,128,128]{3,2,1,0:T(8,128)(2,1)S(1)}, bf16[4,2,128,128]{3,2,1,0:T(8,128)(2,1)S(1)}, u32[]{:S(2)}, u32[]{:S(2)}) collective-permute-start(bf16[4,2,128,128]{3,2,1,0:T(8,128)(2,1)S(1)} %pad_maximum_fusion.2), channel_id=1, source_target_pairs={{0,24},{1,25},{2,26},{3,27},{4,28},{5,29},{6,30},{7,31},{8,0},{9,1... | collective-permute-start | bytes 786440 | tf_op jit(solution)/shard_map/ppermute | solution.py:45
  65.3 12.2 %collective-permute-start.6 = (bf16[4,2,128,128]{3,2,1,0:T(8,128)(2,1)S(1)}, bf16[4,2,128,128]{3,2,1,0:T(8,128)(2,1)S(1)}, u32[]{:S(2)}, u32[]{:S(2)}) collective-permute-start(bf16[4,2,128,128]{3,2,1,0:T(8,128)(2,1)S(1)} %pad_maximum_fusion.2), channel_id=1, source_target_pairs={{0,8},{1,9},{2,10},{3,11},{4,12},{5,13},{6,14},{7,15},{8,16},{9,17... | collective-permute-start | bytes 786440 | tf_op jit(solution)/shard_map/ppermute | solution.py:45
  113.8 11.9 %collective-permute-start.17 = (bf16[256,768]{1,0:T(8,128)(2,1)S(1)}, bf16[256,768]{1,0:T(8,128)(2,1)S(1)}, u32[]{:S(2)}, u32[]{:S(2)}) collective-permute-start(bf16[256,768]{1,0:T(8,128)(2,1)S(1)} %out_projection.2.v0), channel_id=1, source_target_pairs={{0,64},{1,65},{2,66},{3,67},{4,68},{5,69},{6,70},{7,71},{8,72},{9,... | collective-permute-start | bytes 1179656 | tf_op jit(solution)/shard_map/ppermute | solution.py:45
  115.0 11.9 %collective-permute-start.16 = (bf16[256,768]{1,0:T(8,128)(2,1)S(1)}, bf16[256,768]{1,0:T(8,128)(2,1)S(1)}, u32[]{:S(2)}, u32[]{:S(2)}) collective-permute-start(bf16[256,768]{1,0:T(8,128)(2,1)S(1)} %out_projection.2.v0), channel_id=1, source_target_pairs={{0,32},{1,33},{2,34},{3,35},{4,36},{5,37},{6,38},{7,39},{8,40},{9,... | collective-permute-start | bytes 1179656 | tf_op jit(solution)/shard_map/ppermute | solution.py:45
  157.5 9.6 %collective-permute-start.26 = (bf16[2,2,128,128]{3,2,1,0:T(8,128)(2,1)S(1)}, bf16[2,2,128,128]{3,2,1,0:T(8,128)(2,1)S(1)}, u32[]{:S(2)}, u32[]{:S(2)}) collective-permute-start(bf16[2,2,128,128]{3,2,1,0:T(8,128)(2,1)S(1)} %get-tuple-element.58), channel_id=1, source_target_pairs={{0,16},{1,17},{2,18},{3,19},{4,20},{5,21},{6,22},{7,23},{8,24},{9,... | collective-permute-start | bytes 393224 | tf_op jit(solution)/shard_map/ppermute | solution.py:45
  159.0 8.0 %collective-permute-start.25 = (bf16[2,2,128,128]{3,2,1,0:T(8,128)(2,1)S(1)}, bf16[2,2,128,128]{3,2,1,0:T(8,128)(2,1)S(1)}, u32[]{:S(2)}, u32[]{:S(2)}) collective-permute-start(bf16[2,2,128,128]{3,2,1,0:T(8,128)(2,1)S(1)} %get-tuple-element.58), channel_id=1, source_target_pairs={{0,24},{1,25},{2,26},{3,27},{4,28},{5,29},{6,30},{7,31},{8,0},{9,1... | collective-permute-start | bytes 393224 | tf_op jit(solution)/shard_map/ppermute | solution.py:45
  160.7 6.3 %collective-permute-start.24 = (bf16[2,2,128,128]{3,2,1,0:T(8,128)(2,1)S(1)}, bf16[2,2,128,128]{3,2,1,0:T(8,128)(2,1)S(1)}, u32[]{:S(2)}, u32[]{:S(2)}) collective-permute-start(bf16[2,2,128,128]{3,2,1,0:T(8,128)(2,1)S(1)} %get-tuple-element.58), channel_id=1, source_target_pairs={{0,8},{1,9},{2,10},{3,11},{4,12},{5,13},{6,14},{7,15},{8,16},{9,17... | collective-permute-start | bytes 393224 | tf_op jit(solution)/shard_map/ppermute | solution.py:45
  160.7 5.4 %collective-permute-start.20 = (bf16[2,2,128,128]{3,2,1,0:T(8,128)(2,1)S(1)}, bf16[2,2,128,128]{3,2,1,0:T(8,128)(2,1)S(1)}, u32[]{:S(2)}, u32[]{:S(2)}) collective-permute-start(bf16[2,2,128,128]{3,2,1,0:T(8,128)(2,1)S(1)} %get-tuple-element.59), channel_id=1, source_target_pairs={{0,2},{1,3},{2,0},{3,1},{4,6},{5,7},{6,4},{7,5},{8,10},{9,11},{10,... | collective-permute-start | bytes 393224 | tf_op jit(solution)/shard_map/ppermute | solution.py:45
  167.1 7.9 %collective-permute-start.28 = (bf16[12,2,128,128]{3,2,1,0:T(8,128)(2,1)S(1)}, bf16[12,2,128,128]{3,2,1,0:T(8,128)(2,1)S(1)}, u32[]{:S(2)}, u32[]{:S(2)}) collective-permute-start(bf16[12,2,128,128]{3,2,1,0:T(8,128)(2,1)S(1)} %constant_dynamic-update-slice_fusion.8.refs_2_), channel_id=1, source_target_pairs={{0,32},{1,33},{2,34},{3,35},{4,36},{5,37},{6,38},{7,39},{8,40},{9,... | collective-permute-start | bytes 2359304 | tf_op jit(solution)/shard_map/ppermute | solution.py:45
  170.1 16.7 %collective-permute-start.27 = (bf16[8,2,128,128]{3,2,1,0:T(8,128)(2,1)S(1)}, bf16[8,2,128,128]{3,2,1,0:T(8,128)(2,1)S(1)}, u32[]{:S(2)}, u32[]{:S(2)}) collective-permute-start(bf16[8,2,128,128]{3,2,1,0:T(8,128)(2,1)S(1)} %pad_maximum_fusion.1), channel_id=1, source_target_pairs={{0,2},{1,3},{2,0},{3,1},{4,6},{5,7},{6,4},{7,5},{8,10},{9,11},{10,... | collective-permute-start | bytes 1572872 | tf_op jit(solution)/shard_map/ppermute | solution.py:45
  171.4 13.3 %collective-permute-start.23 = (bf16[4,2,128,128]{3,2,1,0:T(8,128)(2,1)S(1)}, bf16[4,2,128,128]{3,2,1,0:T(8,128)(2,1)S(1)}, u32[]{:S(2)}, u32[]{:S(2)}) collective-permute-start(bf16[4,2,128,128]{3,2,1,0:T(8,128)(2,1)S(1)} %pad_maximum_fusion.3), channel_id=1, source_target_pairs={{0,16},{1,17},{2,18},{3,19},{4,20},{5,21},{6,22},{7,23},{8,24},{9,... | collective-permute-start | bytes 786440 | tf_op jit(solution)/shard_map/ppermute | solution.py:45
  173.1 13.7 %collective-permute-start.22 = (bf16[4,2,128,128]{3,2,1,0:T(8,128)(2,1)S(1)}, bf16[4,2,128,128]{3,2,1,0:T(8,128)(2,1)S(1)}, u32[]{:S(2)}, u32[]{:S(2)}) collective-permute-start(bf16[4,2,128,128]{3,2,1,0:T(8,128)(2,1)S(1)} %pad_maximum_fusion.3), channel_id=1, source_target_pairs={{0,24},{1,25},{2,26},{3,27},{4,28},{5,29},{6,30},{7,31},{8,0},{9,1... | collective-permute-start | bytes 786440 | tf_op jit(solution)/shard_map/ppermute | solution.py:45
  174.7 12.1 %collective-permute-start.21 = (bf16[4,2,128,128]{3,2,1,0:T(8,128)(2,1)S(1)}, bf16[4,2,128,128]{3,2,1,0:T(8,128)(2,1)S(1)}, u32[]{:S(2)}, u32[]{:S(2)}) collective-permute-start(bf16[4,2,128,128]{3,2,1,0:T(8,128)(2,1)S(1)} %pad_maximum_fusion.3), channel_id=1, source_target_pairs={{0,8},{1,9},{2,10},{3,11},{4,12},{5,13},{6,14},{7,15},{8,16},{9,17... | collective-permute-start | bytes 786440 | tf_op jit(solution)/shard_map/ppermute | solution.py:45
  223.7 6.7 %collective-permute-start.33 = (bf16[64,768]{1,0:T(8,128)(2,1)S(1)}, bf16[64,768]{1,0:T(8,128)(2,1)S(1)}, u32[]{:S(2)}, u32[]{:S(2)}) collective-permute-start(bf16[64,768]{1,0:T(8,128)(2,1)S(1)} %get-tuple-element.62), channel_id=1, source_target_pairs={{0,96},{1,97},{2,98},{3,99},{4,100},{5,101},{6,102},{7,103},{8,104... | collective-permute-start | bytes 294920 | tf_op jit(solution)/shard_map/ppermute | solution.py:45
  225.2 6.9 %collective-permute-start.32 = (bf16[64,768]{1,0:T(8,128)(2,1)S(1)}, bf16[64,768]{1,0:T(8,128)(2,1)S(1)}, u32[]{:S(2)}, u32[]{:S(2)}) collective-permute-start(bf16[64,768]{1,0:T(8,128)(2,1)S(1)} %get-tuple-element.63), channel_id=1, source_target_pairs={{0,64},{1,65},{2,66},{3,67},{4,68},{5,69},{6,70},{7,71},{8,72},{9,... | collective-permute-start | bytes 294920 | tf_op jit(solution)/shard_map/ppermute | solution.py:45
  (21 other events, 270.6 us)
